TPU v7x, 256 devices: a whole 4x4x8 slice. The times are simulated.
256 devices in a mesh: ctx: 4 (over x), head: 32 (over z, y), rep: 2 (over core).
Axes of the slice: x: 4, y: 4, z: 8, core: 2. Of those that a mesh axis runs over, the one named last changes fastest.
Arguments:
- queries: bfloat16 [1024, 16384], P(('rep', 'ctx'), 'head'), parts along dimension 0, may hold values from -16 to 16
- history_keys: bfloat16 [32768, 1024], P(('rep', 'ctx')), parts along dimension 0, may hold values from -8 to 8
- history_values: bfloat16 [32768, 1024], P(('rep', 'ctx')), parts along dimension 0, may hold values from -6 to 6
- new_keys: bfloat16 [1024, 1024], P(('rep', 'ctx')), parts along dimension 0, may hold values from -6 to 6
- new_values: bfloat16 [1024, 1024], P(('rep', 'ctx')), parts along dimension 0, may hold values from -6 to 6
- shard_lengths: int32 [8], P(('rep', 'ctx')), parts along dimension 0, may hold values from 1 to 4096, 10240 in all
- positions: int32 [1024], P('rep'), parts along dimension 0, may hold values from 0 to 511, each once
- out_weight: bfloat16 [16384, 16384], P('head', 'ctx'), may hold values from -0.75 to 0.75
Outputs:
- mixed: bfloat16 [1024, 16384], P(('rep', 'head'), 'ctx'), parts along dimension 0
There are 2 independent parts, one for each index of `rep`. A program takes and returns all parts, laid end to end along the dimension named above; an argument that names none is the same for every part. Nothing has to cross between parts.
All inputs are finite; a program needn't handle non-finite values. No bound on the sum of `shard_lengths` on one device may be relied on, other than what follows from the above.
Results may differ from a plain program's by a relative error of at most 0.0054.
Values may be sent and summed in bfloat16 or wider, within the bound.
No kernel may reach another device: no remote copies, remote signals or barrier semaphores. Data moves between devices by JAX's collectives and lax.ppermute only.
A program may use at most 128 MiB of HBM per device.

v0:
```python
import jax
import jax.numpy as jnp
from jax import lax
from jax.sharding import PartitionSpec as P

HD = 128
GROUP = 16
TILE = 512


neg_fill = -1e30


def combine_states(first, second):
    out_a, top_a, sum_a = first
    out_b, top_b, sum_b = second
    peak_top = jnp.maximum(top_a, top_b)
    scale_a = jnp.exp(top_a - peak_top)
    scale_b = jnp.exp(top_b - peak_top)
    return (
        out_a * scale_a[..., None] + out_b * scale_b[..., None],
        peak_top,
        sum_a * scale_a + sum_b * scale_b,
    )


def shards(
    queries,
    history_keys,
    history_values,
    new_keys,
    new_values,
    shard_lengths,
    positions,
    out_weight,
):
    head_count = queries.shape[1] // HD
    group_dev = min(head_count, GROUP)
    kv_per = head_count // group_dev
    kv_start = lax.axis_index("head") * head_count // GROUP
    gathered = lax.all_gather(queries, "ctx", axis=0, tiled=True)
    row_count = gathered.shape[0]
    queried = gathered.reshape(row_count, kv_per, group_dev, HD)
    own_index = lax.axis_index("ctx")
    live_count = shard_lengths[0]
    score_scale = HD ** (-0.5)

    def add_block(carried, key_tile, value_tile, visible):
        scores = (
            jnp.einsum("qgjd,kgd->qgjk", queried, key_tile, preferred_element_type=jnp.float32)
            * score_scale
        )
        key_mask = visible[:, None, None, :]
        scores = jnp.where(key_mask, scores, neg_fill)
        block_top = jnp.max(scores, axis=-1)
        weights = jnp.where(key_mask, jnp.exp(scores - block_top[..., None]), 0.0).astype(
            jnp.bfloat16
        )
        block_sum = jnp.sum(weights.astype(jnp.float32), axis=-1)
        block_out = jnp.einsum(
            "qgjk,kgd->qgjd", weights, value_tile, preferred_element_type=jnp.float32
        )
        return combine_states(carried, (block_out, block_top, block_sum))

    initial = (
        jnp.zeros((row_count, kv_per, group_dev, HD), jnp.float32),
        jnp.full((row_count, kv_per, group_dev), neg_fill, jnp.float32),
        jnp.zeros((row_count, kv_per, group_dev), jnp.float32),
    )
    hist_keys = lax.dynamic_slice_in_dim(history_keys, kv_start * HD, kv_per * HD, 1).reshape(
        -1, kv_per, HD
    )
    hist_values = lax.dynamic_slice_in_dim(history_values, kv_start * HD, kv_per * HD, 1).reshape(
        -1, kv_per, HD
    )
    tile_total = hist_keys.shape[0] // TILE

    def tile_step(tile_index, carried):
        tile_start = tile_index * TILE
        key_tile = lax.dynamic_slice_in_dim(hist_keys, tile_start, TILE, 0)
        value_tile = lax.dynamic_slice_in_dim(hist_values, tile_start, TILE, 0)
        slot_ids = tile_start + jnp.arange(TILE, dtype=jnp.int32)
        return add_block(carried, key_tile, value_tile, (slot_ids < live_count)[None, :])

    carried = lax.fori_loop(0, tile_total, tile_step, initial)
    new_count = new_keys.shape[0]
    own_new_keys = lax.dynamic_slice_in_dim(new_keys, kv_start * HD, kv_per * HD, 1).reshape(
        new_count, kv_per, HD
    )
    own_new_values = lax.dynamic_slice_in_dim(new_values, kv_start * HD, kv_per * HD, 1).reshape(
        new_count, kv_per, HD
    )
    local_pos = lax.dynamic_slice_in_dim(positions, own_index * new_count, new_count, 0)
    visible_new = local_pos[None, :] <= positions[:, None]
    carried = add_block(carried, own_new_keys, own_new_values, visible_new)
    state_out, state_top, state_sum = carried
    flat_out = state_out.reshape(row_count, head_count * HD)
    flat_top = state_top.reshape(row_count, head_count)
    flat_sum = state_sum.reshape(row_count, head_count)
    returned = (
        lax.all_to_all(flat_out[None], "ctx", split_axis=1, concat_axis=0, tiled=True),
        lax.all_to_all(flat_top[None], "ctx", split_axis=1, concat_axis=0, tiled=True),
        lax.all_to_all(flat_sum[None], "ctx", split_axis=1, concat_axis=0, tiled=True),
    )
    outs_back, tops_back, sums_back = returned
    peak_top = jnp.max(tops_back, axis=0)
    weight_back = jnp.exp(tops_back - peak_top[None])
    owned_rows = outs_back.shape[1]
    numerator = jnp.sum(
        outs_back.reshape(outs_back.shape[0], owned_rows, head_count, HD) * weight_back[..., None],
        axis=0,
    )
    denominator = jnp.sum(sums_back * weight_back, axis=0)
    attn_own = (
        (numerator / denominator[..., None])
        .reshape(owned_rows, head_count * HD)
        .astype(jnp.bfloat16)
    )
    partial_sum = jnp.dot(
        lax.all_gather(attn_own, "ctx", axis=0, tiled=True),
        out_weight,
        preferred_element_type=jnp.float32,
    )
    mixed = lax.psum_scatter(partial_sum, "head", scatter_dimension=0, tiled=True).astype(
        jnp.bfloat16
    )
    return mixed


def solution(mesh):
    in_specs = (
        P(("rep", "ctx"), "head"),
        P(("rep", "ctx"), None),
        P(("rep", "ctx"), None),
        P(("rep", "ctx"), None),
        P(("rep", "ctx"), None),
        P(("rep", "ctx")),
        P("rep"),
        P("head", "ctx"),
    )
    out_specs = P(("rep", "head"), "ctx")
    return jax.shard_map(shards, mesh=mesh, in_specs=in_specs, out_specs=out_specs, check_vma=False)
```

profile of v0, /device:TPU:16, one launch (start us, length us, event | category | flops | bytes accessed | tf_op | source)
XLA Modules:
  0.0 394.7 jit_solution(15804352285944256408)
XLA Ops:
  9.9 14.4 %all_gather.6 = bf16[512,512]{0,1:T(8,128)(2,1)S(1)} all-gather(bf16[128,512]{0,1:T(8,128)(2,1)S(1)} %copy.39), channel_id=1, replica_groups=mesh['ctx'=4,'head'=32,'rep'=2] {'ctx'}, dimensions={0}, use_global_device_ids=true | all-gather | bytes 655360 | tf_op jit(solution)/shard_map/all_gather | solution.py:41
  24.5 74.1 %while.18 = (s32[]{:T(128)}, f32[512,1,4,128]{0,3,2,1:T(8,128)}, f32[512,1,4]{0,2,1:T(4,128)S(1)}, f32[512,1,4]{0,2,1:T(4,128)S(1)}, s32[]{:T(128)}, /*index=5*/...) while((s32[]{:T(128)}, f32[512,1,4,128]{0,3,2,1:T(8,128)}, ...), condition=%wide.region_3.4_spmd.clone, body=%wide.region_0.3_spmd.clone.sunk | while | flops 553667584 | bytes 32402136 | solution.py:85
  26.0 1.9 copy-done.1
  29.1 4.4 %fusion.68 = f32[512,1,4,128]{0,3,2,1:T(8,128)} fusion(f32[512,1,4,128]{0,3,2,1:T(8,128)} %get-tuple-element.304, f32[512,4]{0,1:T(4,128)S(1)} %get-tuple-element.288, f32[512,4]{0,1:T(4,128)S(1)} %get-tuple-element.289, pred[]{:T(512)S(6)} %compare.5, bf16[4096,1,128]{0,2,1:T(8,128)(2,1)S(1)} %get-tuple-element.322, s32[]{:T(128)S(6)} %select_n.92, ...), kind=kOutput, calls=%fused_computation.12.clone.1 | convolution fusion | flops 274726912 | bytes 6448133 | tf_op jit(solution)/shard_map/while/body/eval_jaxpr/qgjk,kgd->qgjd/dot_general | solution.py:60
  34.9 1.9 copy-done.1
  38.1 4.7 %fusion.68 = f32[512,1,4,128]{0,3,2,1:T(8,128)} fusion(f32[512,1,4,128]{0,3,2,1:T(8,128)} %get-tuple-element.304, f32[512,4]{0,1:T(4,128)S(1)} %get-tuple-element.288, f32[512,4]{0,1:T(4,128)S(1)} %get-tuple-element.289, pred[]{:T(512)S(6)} %compare.5, bf16[4096,1,128]{0,2,1:T(8,128)(2,1)S(1)} %get-tuple-element.322, s32[]{:T(128)S(6)} %select_n.92, ...), kind=kOutput, calls=%fused_computation.12.clone.1 | convolution fusion | flops 274726912 | bytes 6448133 | tf_op jit(solution)/shard_map/while/body/eval_jaxpr/qgjk,kgd->qgjd/dot_general | solution.py:60
  47.4 4.7 %fusion.68 = f32[512,1,4,128]{0,3,2,1:T(8,128)} fusion(f32[512,1,4,128]{0,3,2,1:T(8,128)} %get-tuple-element.304, f32[512,4]{0,1:T(4,128)S(1)} %get-tuple-element.288, f32[512,4]{0,1:T(4,128)S(1)} %get-tuple-element.289, pred[]{:T(512)S(6)} %compare.5, bf16[4096,1,128]{0,2,1:T(8,128)(2,1)S(1)} %get-tuple-element.322, s32[]{:T(128)S(6)} %select_n.92, ...), kind=kOutput, calls=%fused_computation.12.clone.1 | convolution fusion | flops 274726912 | bytes 6448133 | tf_op jit(solution)/shard_map/while/body/eval_jaxpr/qgjk,kgd->qgjd/dot_general | solution.py:60
  53.5 1.9 copy-done.1
  56.7 4.7 %fusion.68 = f32[512,1,4,128]{0,3,2,1:T(8,128)} fusion(f32[512,1,4,128]{0,3,2,1:T(8,128)} %get-tuple-element.304, f32[512,4]{0,1:T(4,128)S(1)} %get-tuple-element.288, f32[512,4]{0,1:T(4,128)S(1)} %get-tuple-element.289, pred[]{:T(512)S(6)} %compare.5, bf16[4096,1,128]{0,2,1:T(8,128)(2,1)S(1)} %get-tuple-element.322, s32[]{:T(128)S(6)} %select_n.92, ...), kind=kOutput, calls=%fused_computation.12.clone.1 | convolution fusion | flops 274726912 | bytes 6448133 | tf_op jit(solution)/shard_map/while/body/eval_jaxpr/qgjk,kgd->qgjd/dot_general | solution.py:60
  62.8 1.9 copy-done.1
  66.0 4.7 %fusion.68 = f32[512,1,4,128]{0,3,2,1:T(8,128)} fusion(f32[512,1,4,128]{0,3,2,1:T(8,128)} %get-tuple-element.304, f32[512,4]{0,1:T(4,128)S(1)} %get-tuple-element.288, f32[512,4]{0,1:T(4,128)S(1)} %get-tuple-element.289, pred[]{:T(512)S(6)} %compare.5, bf16[4096,1,128]{0,2,1:T(8,128)(2,1)S(1)} %get-tuple-element.322, s32[]{:T(128)S(6)} %select_n.92, ...), kind=kOutput, calls=%fused_computation.12.clone.1 | convolution fusion | flops 274726912 | bytes 6448133 | tf_op jit(solution)/shard_map/while/body/eval_jaxpr/qgjk,kgd->qgjd/dot_general | solution.py:60
  72.1 1.9 copy-done.1
  75.3 4.7 %fusion.68 = f32[512,1,4,128]{0,3,2,1:T(8,128)} fusion(f32[512,1,4,128]{0,3,2,1:T(8,128)} %get-tuple-element.304, f32[512,4]{0,1:T(4,128)S(1)} %get-tuple-element.288, f32[512,4]{0,1:T(4,128)S(1)} %get-tuple-element.289, pred[]{:T(512)S(6)} %compare.5, bf16[4096,1,128]{0,2,1:T(8,128)(2,1)S(1)} %get-tuple-element.322, s32[]{:T(128)S(6)} %select_n.92, ...), kind=kOutput, calls=%fused_computation.12.clone.1 | convolution fusion | flops 274726912 | bytes 6448133 | tf_op jit(solution)/shard_map/while/body/eval_jaxpr/qgjk,kgd->qgjd/dot_general | solution.py:60
  84.5 4.7 %fusion.68 = f32[512,1,4,128]{0,3,2,1:T(8,128)} fusion(f32[512,1,4,128]{0,3,2,1:T(8,128)} %get-tuple-element.304, f32[512,4]{0,1:T(4,128)S(1)} %get-tuple-element.288, f32[512,4]{0,1:T(4,128)S(1)} %get-tuple-element.289, pred[]{:T(512)S(6)} %compare.5, bf16[4096,1,128]{0,2,1:T(8,128)(2,1)S(1)} %get-tuple-element.322, s32[]{:T(128)S(6)} %select_n.92, ...), kind=kOutput, calls=%fused_computation.12.clone.1 | convolution fusion | flops 274726912 | bytes 6448133 | tf_op jit(solution)/shard_map/while/body/eval_jaxpr/qgjk,kgd->qgjd/dot_general | solution.py:60
  93.8 4.7 %fusion.68 = f32[512,1,4,128]{0,3,2,1:T(8,128)} fusion(f32[512,1,4,128]{0,3,2,1:T(8,128)} %get-tuple-element.304, f32[512,4]{0,1:T(4,128)S(1)} %get-tuple-element.288, f32[512,4]{0,1:T(4,128)S(1)} %get-tuple-element.289, pred[]{:T(512)S(6)} %compare.5, bf16[4096,1,128]{0,2,1:T(8,128)(2,1)S(1)} %get-tuple-element.322, s32[]{:T(128)S(6)} %select_n.92, ...), kind=kOutput, calls=%fused_computation.12.clone.1 | convolution fusion | flops 274726912 | bytes 6448133 | tf_op jit(solution)/shard_map/while/body/eval_jaxpr/qgjk,kgd->qgjd/dot_general | solution.py:60
  102.2 3.3 all-to-all-start.1
  107.8 3.0 all-to-all-done.1
  110.9 3.2 all-to-all-start.2
  115.7 1.9 copy.45
  119.4 3.5 all-to-all-start
  125.8 8.0 %all-to-all-done = f32[1,512,512]{2,0,1:T(1,128)S(1)} async-done(((f32[1,512,512]{2,0,1:T(1,128)}), f32[1,512,512]{2,0,1:T(1,128)S(1)}, u32[]{:S(2)}, u32[]{:S(2)}) %all-to-all-start) | async-done | bytes 1048608 | tf_op jit(solution)/shard_map/all_to_all | solution.py:101
  135.9 12.0 %all_gather.7 = bf16[512,512]{0,1:T(8,128)(2,1)S(1)} all-gather(bf16[128,512]{0,1:T(8,128)(2,1)S(1)} %fusion.40), channel_id=1, replica_groups=mesh['ctx'=4,'head'=32,'rep'=2] {'ctx'}, dimensions={0}, use_global_device_ids=true | all-gather | bytes 655360 | tf_op jit(solution)/shard_map/all_gather | solution.py:120
  148.0 7.8 %fusion.55 = f32[512,4096]{1,0:T(8,128)} fusion(bf16[512,512]{0,1:T(8,128)(2,1)S(1)} %all_gather.7, bf16[512,4096]{1,0:T(8,128)(2,1)} %param.17), kind=kOutput, calls=%fused_computation.72 | convolution fusion | flops 2147483648 | bytes 13107200 | tf_op jit(solution)/shard_map/dot_general | solution.py:119
  155.8 230.4 %reduce-scatter.2.cloned.1.call-done = f32[16,4096]{1,0:T(8,128)} async-done(((f32[512,4096]{1,0:T(8,128)}), f32[16,4096]{1,0:T(8,128)}) %reduce-scatter.2.cloned.1.call-update) | async-done | bytes 262160 | tf_op jit(solution)/shard_map/reduce_scatter | solution.py:124
  (102 shorter events, 45.9 us)
Async XLA Ops:
  6.5 92.2 %copy-start = (bf16[128,1024]{1,0:T(8,128)(2,1)S(1)}, bf16[128,1024]{1,0:T(8,128)(2,1)}, u32[]{:S(2)}) copy-start(bf16[128,1024]{1,0:T(8,128)(2,1)} %param.13) | copy-start | bytes 786436
  6.5 3.2 copy-start.2
  24.5 74.1 %copy-start.3 = (s32[512]{0:T(512)S(1)}, s32[512]{0:T(512)}, u32[]{:S(2)}) copy-start(s32[512]{0:T(512)} %param.16) | copy-start | bytes 6148
  25.9 1.9 copy-start.1
  34.9 1.9 copy-start.1
  44.2 1.9 copy-start.1
  53.5 1.9 copy-start.1
  62.8 1.9 copy-start.1
  72.1 1.9 copy-start.1
  81.4 1.9 copy-start.1
  90.7 1.9 copy-start.1
  102.2 8.6 %all-to-all-start.1 = ((f32[4,1,512]{2,1,0:T(1,128)}), f32[4,1,512]{2,1,0:T(1,128)S(1)}, u32[]{:S(2)}, u32[]{:S(2)}) async-start(f32[4,1,512]{2,1,0:T(1,128)} %reshape.180), calls=%async_computation.1 | async-start | bytes 16384 | tf_op jit(solution)/shard_map/all_to_all | solution.py:102
  110.9 8.5 %all-to-all-start.2 = ((f32[4,1,512]{2,1,0:T(1,128)}), f32[4,1,512]{2,1,0:T(1,128)S(1)}, u32[]{:S(2)}, u32[]{:S(2)}) async-start(f32[4,1,512]{2,1,0:T(1,128)} %reshape.182), calls=%async_computation.2 | async-start | bytes 16384 | tf_op jit(solution)/shard_map/all_to_all | solution.py:103
  119.4 14.4 %all-to-all-start = ((f32[1,512,512]{2,0,1:T(1,128)}), f32[1,512,512]{2,0,1:T(1,128)S(1)}, u32[]{:S(2)}, u32[]{:S(2)}) async-start(f32[1,512,512]{2,0,1:T(1,128)} %copy.45), calls=%async_computation | async-start | bytes 2097152 | tf_op jit(solution)/shard_map/all_to_all | solution.py:101
  122.9 263.3 %reduce-scatter.2.cloned.1.call-start = ((), (), s32[]{:S(2)}) async-start(), calls=%async_computation.4 | async-start | bytes 8650752 | tf_op jit(solution)/shard_map/reduce_scatter | solution.py:124
Sparse Core Ops, SparseCore 0:
  155.9 230.2 reduce-scatter.1
where the time goes:
time: 396 us; the launch traced here: 395 us
  waiting for transfers between devices  243 us (61%)
  matrix products  53.3 us (13%)
  blocking collectives  26.4 us (7%)
  local copies, waits for them, and re-layouts  26 us (7%)
  other arithmetic  21.7 us (5%)
  between operations  13.6 us (3%)
  starting transfers between devices  10.1 us (3%)
    reduce_scatter x1, waiting for transfers between devices, shards(): lax.psum_scatter(partial_sum, 'head', scatter_dimension=0, tiled=True)  230 us
    dot_general x9, matrix products, add_block(): jnp.einsum('qgjk,kgd->qgjd', weights, value_tile, preferred_element_type=...  39.2 us
    while x24, local copies, waits for them, and re-layouts  15.4 us
    all_gather x1, blocking collectives, shards(): gathered = lax.all_gather(queries, 'ctx', axis=0, tiled=True)  14.4 us
    all_gather x1, blocking collectives, shards(): lax.all_gather(attn_own, 'ctx', axis=0, tiled=True)  12 us
    reduce_sum x9, other arithmetic, add_block(): block_sum = jnp.sum(weights.astype(jnp.float32), axis=-1)  9.5 us
    all_to_all x1, waiting for transfers between devices, shards(): lax.all_to_all(flat_out[None], 'ctx', split_axis=1, concat_axis=0, tiled=...  8.04 us
  transfers between devices with their start and end apart: 4, of which 4 were waited for; matrix products, arithmetic and copies ran while one was open for 2% of the time, Pallas kernels for 0%

commit v1 on v0

v1 whole, which is shorter than its diff:
```python
import functools

import jax
import jax.numpy as jnp
from jax import lax
from jax.experimental import pallas as pl
from jax.experimental.pallas import tpu as pltpu
from jax.sharding import Mesh
from jax.sharding import PartitionSpec as P

HD = 128
GROUP = 16
NEG = -1e30
VMEM = 56 << 20


def shift(x, axis, size, by):
    return lax.ppermute(x, axis, [(i, (i + by) % size) for i in range(size)])


def attn_kernel(blocks, first, tok, heads, tile, steps, n_ctx, scalars, *refs):
    q_refs = refs[:blocks]
    k_ref, v_ref, nk_ref, nv_ref, pos_ref = refs[blocks : blocks + 5]
    outs = refs[blocks + 5 : 2 * blocks + 5]
    q_s, top_s, acc_s = refs[2 * blocks + 5 :]
    step = pl.program_id(0)
    live = scalars[0]
    ctx = scalars[2]
    rows = tok * heads

    @pl.when(step == 0)
    def _():
        for b in range(blocks):
            for h in range(heads):
                q_s[pl.ds(b * rows + h * tok, tok), :] = q_refs[b][:, h * HD : (h + 1) * HD]
        top_s[...] = jnp.full(top_s.shape, NEG, jnp.float32)
        acc_s[...] = jnp.zeros(acc_s.shape, jnp.float32)

    def add(b, keys, values, mask):
        own = pl.ds(b * rows, rows)
        scores = lax.dot_general(
            q_s[own, :], keys, (((1,), (1,)), ((), ())), preferred_element_type=jnp.float32
        )
        scores = scores * (HD**-0.5)
        if mask is not None:
            scores = jnp.where(mask(b, scores.shape), scores, NEG)
        old = top_s[own, :]
        new = jnp.maximum(old, jnp.max(scores, axis=1, keepdims=True))
        weights = jnp.exp(scores - new[:, :1]).astype(jnp.bfloat16)
        scale = jnp.exp(old - new)
        both = jnp.concatenate([values, jnp.ones_like(values)], axis=1)
        part = jnp.dot(weights, both, preferred_element_type=jnp.float32)
        acc_s[own, :] = acc_s[own, :] * jnp.concatenate([scale, scale], axis=1) + part
        top_s[own, :] = new

    @pl.when((step + 1) * tile <= live)
    def _():
        for b in range(blocks):
            add(b, k_ref[...], v_ref[...], None)

    @pl.when(((step + 1) * tile > live) & (step * tile < live))
    def _():
        def mask(b, shape):
            return step * tile + lax.broadcasted_iota(jnp.int32, shape, 1) < live

        for b in range(blocks):
            add(b, k_ref[...], v_ref[...], mask)

    @pl.when(step == steps - 1)
    def _():
        key_pos = jnp.broadcast_to(pos_ref[pl.ds(ctx, 1), :], (tok, tok))

        def mask(b, shape):
            row = pos_ref[pl.ds(lax.rem(ctx + n_ctx - first - b, n_ctx), 1), :]
            seen = key_pos <= jnp.broadcast_to(row, (tok, tok)).T
            return jnp.concatenate([seen] * heads, axis=0)

        for b in range(blocks):
            add(b, nk_ref[...], nv_ref[...], mask)
        lane = lax.broadcasted_iota(jnp.int32, (tok, HD), 1)
        for b in range(blocks):
            stats = jnp.zeros((tok, HD), jnp.float32)
            for h in range(heads):
                own = pl.ds(b * rows + h * tok, tok)
                total = acc_s[own, HD:]
                outs[b][:, h * HD : (h + 1) * HD] = (acc_s[own, :HD] / total).astype(jnp.bfloat16)
                level = top_s[own, :] + jnp.log(total)
                high = level.astype(jnp.bfloat16).astype(jnp.float32)
                middle = (level - high).astype(jnp.bfloat16).astype(jnp.float32)
                low = level - high - middle
                stats = jnp.where(lane == 3 * h, high, stats)
                stats = jnp.where(lane == 3 * h + 1, middle, stats)
                stats = jnp.where(lane == 3 * h + 2, low, stats)
            outs[b][:, heads * HD :] = stats.astype(jnp.bfloat16)


def attend(queries, first, keys, values, new_keys, new_values, pos, scalars):
    blocks = len(queries)
    tok, width = queries[0].shape
    heads = width // HD
    tile = min(2048, keys.shape[0])
    steps = keys.shape[0] // tile
    n_ctx = pos.shape[0]
    whole = lambda shape: pl.BlockSpec(shape, lambda i, s: (0, 0))
    hist = pl.BlockSpec((tile, HD), lambda i, s: (jnp.minimum(i, (s[0] - 1) // tile), s[1]))
    new = pl.BlockSpec((new_keys.shape[0], HD), lambda i, s: (0, s[1]))
    total = blocks * tok * heads
    return pl.pallas_call(
        functools.partial(attn_kernel, blocks, first, tok, heads, tile, steps, n_ctx),
        grid_spec=pltpu.PrefetchScalarGridSpec(
            num_scalar_prefetch=1,
            grid=(steps,),
            in_specs=[whole((tok, width))] * blocks + [hist, hist, new, new, whole(pos.shape)],
            out_specs=[whole((tok, width + HD))] * blocks,
            scratch_shapes=[
                pltpu.VMEM((total, HD), jnp.bfloat16),
                pltpu.VMEM((total, HD), jnp.float32),
                pltpu.VMEM((total, 2 * HD), jnp.float32),
            ],
        ),
        out_shape=[jax.ShapeDtypeStruct((tok, width + HD), jnp.bfloat16)] * blocks,
        compiler_params=pltpu.CompilerParams(vmem_limit_bytes=VMEM),
        cost_estimate=pl.CostEstimate(
            flops=8 * total * keys.shape[0] * HD,
            bytes_accessed=4 * keys.shape[0] * HD,
            transcendentals=total * keys.shape[0],
        ),
        name="attend",
    )(scalars, *queries, keys, values, new_keys, new_values, pos)


def combine_kernel(heads, *refs):
    parts, outs = refs[:-2], refs[-2:]
    tok = parts[0].shape[0]
    for h in range(heads):
        at = heads * HD + 3 * h
        levels = []
        for p in parts:
            pieces = p[:, heads * HD :].astype(jnp.float32)
            j = 3 * h
            level = pieces[:, j : j + 1] + pieces[:, j + 1 : j + 2] + pieces[:, j + 2 : j + 3]
            levels.append(jnp.broadcast_to(level, (tok, HD)))
        top = functools.reduce(jnp.maximum, levels)
        weights = [jnp.exp(level - top) for level in levels]
        total = sum(weights[1:], weights[0])
        own = slice(h * HD, (h + 1) * HD)
        mixed = sum(w * p[:, own].astype(jnp.float32) for w, p in zip(weights, parts))
        done = (mixed / total).astype(jnp.bfloat16)
        outs[0][:, own] = done[: tok // 2]
        outs[1][:, own] = done[tok // 2 :]


def combine(parts):
    tok, width = parts[0].shape
    width -= HD
    return pl.pallas_call(
        functools.partial(combine_kernel, width // HD),
        out_shape=[jax.ShapeDtypeStruct((tok // 2, width), jnp.bfloat16)] * 2,
        compiler_params=pltpu.CompilerParams(vmem_limit_bytes=VMEM),
        name="combine",
    )(*parts)


def project_kernel(n_ctx, n_y, half, scalars, *refs):
    a_refs = refs[:n_y]
    b_refs = refs[n_y : n_y + n_ctx]
    own_ref, near_ref, far_ref, out_ref = refs[n_y + n_ctx :]
    ctx, core = scalars[2], scalars[4]
    feat = own_ref.shape[0]
    cut = feat // 2
    acc = None

    def left(t, cols):
        pieces = [a_refs[t][:, cols]]
        pieces += [b[pl.ds(t * half, half), cols] for b in b_refs]
        return jnp.concatenate(pieces, axis=0)

    def add(acc, lhs, rhs):
        prod = jnp.dot(lhs, rhs, preferred_element_type=jnp.float32)
        return prod if acc is None else acc + prod

    acc = add(acc, left(0, slice(None)), own_ref[...])
    for t in range(1, n_y):
        rows = slice((t - 1) * cut, t * cut)
        mine = pl.ds(pl.multiple_of(core * cut, cut), cut)
        other = pl.ds(pl.multiple_of((1 - core) * cut, cut), cut)
        acc = add(acc, left(t, mine), near_ref[rows, :])
        acc = add(acc, left(t, other), far_ref[rows, :])
    acc = acc.astype(out_ref.dtype)
    for s in range(n_ctx):
        at = lax.rem(ctx + n_ctx - s, n_ctx) * (2 * half)
        for second in range(2):
            piece = (second * n_ctx + s) * half
            place = pl.ds(pl.multiple_of(at + second * half, half), half)
            out_ref[place, :] = acc[piece : piece + half]


def project(a_parts, b_parts, own, near, far, scalars):
    n_y, n_ctx = len(a_parts), len(b_parts)
    rows, feat = a_parts[0].shape
    half = rows // n_ctx
    cols = own.shape[1]
    tile = min(256, cols)
    whole = pl.BlockSpec((rows, feat), lambda i, s: (0, 0))
    other = pl.BlockSpec(b_parts[0].shape, lambda i, s: (0, 0))
    strip = lambda x: pl.BlockSpec((x.shape[0], tile), lambda i, s: (0, i))
    out_rows = 2 * half * n_ctx
    return pl.pallas_call(
        functools.partial(project_kernel, n_ctx, n_y, half),
        grid_spec=pltpu.PrefetchScalarGridSpec(
            num_scalar_prefetch=1,
            grid=(cols // tile,),
            in_specs=[whole] * n_y + [other] * n_ctx + [strip(own), strip(near), strip(far)],
            out_specs=pl.BlockSpec((out_rows, tile), lambda i, s: (0, i)),
        ),
        out_shape=jax.ShapeDtypeStruct((out_rows, cols), jnp.bfloat16),
        compiler_params=pltpu.CompilerParams(vmem_limit_bytes=VMEM),
        cost_estimate=pl.CostEstimate(
            flops=2 * out_rows * feat * n_y * cols, bytes_accessed=7 << 20, transcendentals=0
        ),
        name="project",
    )(scalars, *a_parts, *b_parts, own, near, far)


def shards(
    sizes,
    queries,
    history_keys,
    history_values,
    new_keys,
    new_values,
    shard_lengths,
    positions,
    out_weight,
):
    n_ctx, n_z, n_y, n_rep = sizes
    ctx, z, y, core = (lax.axis_index(a) for a in ("ctx", "z", "y", "rep"))
    kv_head = (z * n_y + y) * (queries.shape[1] // HD) // GROUP
    scalars = jnp.stack([shard_lengths[0], kv_head, ctx, y, core]).astype(jnp.int32)
    pos = positions.reshape(n_ctx, -1)

    feat, all_cols = out_weight.shape
    cols = all_cols // n_y
    cut = feat // n_rep
    with jax.named_scope("weights"):
        near = []
        for t in range(1, n_y):
            to = lax.rem(y + t, n_y)
            block = lax.dynamic_slice(out_weight, (core * cut, to * cols), (cut, cols))
            near.append(shift(block, "y", n_y, t))
        near = jnp.concatenate(near, axis=0)
        far = shift(near, "rep", n_rep, 1)
        own = lax.dynamic_slice(out_weight, (0, y * cols), (feat, cols))

    history = (history_keys, history_values, new_keys, new_values, pos, scalars)
    with jax.named_scope("queries"):
        others = [shift(queries, "ctx", n_ctx, s) for s in range(1, n_ctx)]
    with jax.named_scope("attend"):
        (kept,) = attend([queries], 0, *history)
        sent = attend(others, 1, *history)
    with jax.named_scope("return"):
        back = [shift(p, "ctx", n_ctx, -s) for s, p in enumerate(sent, 1)]
        first, second = combine([kept] + back)
    with jax.named_scope("gather"):
        a = jnp.concatenate(
            [first] + [shift(first, "ctx", n_ctx, s) for s in range(1, n_ctx)], axis=0
        )
        b = jnp.concatenate([second] + [shift(second, "y", n_y, t) for t in range(1, n_y)], axis=0)
        a_parts = [a] + [shift(a, "y", n_y, t) for t in range(1, n_y)]
        b_parts = [b] + [shift(b, "ctx", n_ctx, s) for s in range(1, n_ctx)]
    with jax.named_scope("project"):
        part = project(a_parts, b_parts, own, near, far, scalars)
    with jax.named_scope("reduce"):
        got = lax.all_to_all(part, ("z", "y"), 0, 0, tiled=True)
        got = got.reshape(n_z, n_y, -1, cols).astype(jnp.float32)
        mixed = jnp.sum(got, axis=0).astype(jnp.bfloat16)
        return mixed.transpose(1, 0, 2).reshape(-1, all_cols)


def solution(mesh):
    n_ctx, n_head, n_rep = (mesh.shape[a] for a in ("ctx", "head", "rep"))
    n_y = n_ctx
    n_z = n_head // n_y
    devices = mesh.devices.reshape(n_ctx, n_z, n_y, n_rep)
    fine = Mesh(devices, ("ctx", "z", "y", "rep"))
    head = ("z", "y")
    in_specs = (
        P(("rep", "ctx"), head),
        P(("rep", "ctx"), None),
        P(("rep", "ctx"), None),
        P(("rep", "ctx"), None),
        P(("rep", "ctx"), None),
        P(("rep", "ctx")),
        P("rep"),
        P(head, "ctx"),
    )
    return jax.shard_map(
        functools.partial(shards, (n_ctx, n_z, n_y, n_rep)),
        mesh=fine,
        in_specs=in_specs,
        out_specs=P(("rep", head[0], head[1]), "ctx"),
        check_vma=False,
    )
```

time: 396 us -> 148 us (0.37)
  waiting for transfers between devices: 243 us -> 44.2 us
  matrix products: 53.3 us -> 0 us
  Pallas kernels: 0 us -> 27 us
  starting transfers between devices: 10.1 us -> 33 us
  other arithmetic: 21.7 us -> 0.18 us
  local copies, waits for them, and re-layouts: 26 us -> 11.9 us
  between operations: 13.6 us -> 0.84 us
    reduce_scatter x1 -> x0, waiting for transfers between devices: 230 us -> none  [shards(): lax.psum_scatter(partial_sum, 'head', scatter_dimension=0, tiled=True)]
    dot_general x19 -> x0, matrix products: 53.3 us -> none  [the longest x9 39.2 us: add_block(): jnp.einsum('qgjk,kgd->qgjd', weights, value_tile, preferred_element_type=...]
    ppermute x0 -> x22, waiting for transfers between devices: none -> 44.2 us  [shift(): return lax.ppermute(x, axis, [(i, (i + by) % size) for i in range(size)])]
    ppermute x0 -> x22, starting transfers between devices: none -> 33 us  [shift(): return lax.ppermute(x, axis, [(i, (i + by) % size) for i in range(size)])]
    all_to_all x0 -> x1, blocking collectives: none -> 29.8 us  [shards(): got = lax.all_to_all(part, ('z', 'y'), 0, 0, tiled=True)]
    pallas_call x0 -> x4, Pallas kernels: none -> 27 us  [the longest x2 16.6 us: attend(): pl.pallas_call(functools.partial(attn_kernel, blocks, first, tok, heads,...]
    all_gather x2 -> x0, blocking collectives: 26.4 us -> none  [the longest x1 14.4 us: shards(): gathered = lax.all_gather(queries, 'ctx', axis=0, tiled=True)]
    while x24 -> x0, local copies, waits for them, and re-layouts: 15.4 us -> none
  transfers between devices with their start and end apart: 4 -> 22, of which waited for: 4 -> 10; matrix products, arithmetic and copies ran while one was open for 2% -> 5% of each run, Pallas kernels for 0% -> 14%
where the time goes in v1:
time: 148 us; the launch traced here: 147 us
  waiting for transfers between devices  44.2 us (30%)
  starting transfers between devices  33 us (22%)
  blocking collectives  29.8 us (20%)
  Pallas kernels  27 us (18%)
  local copies, waits for them, and re-layouts  11.9 us (8%)
    ppermute x22, waiting for transfers between devices, shift(): return lax.ppermute(x, axis, [(i, (i + by) % size) for i in range(size)])  44.2 us
    ppermute x22, starting transfers between devices, shift(): return lax.ppermute(x, axis, [(i, (i + by) % size) for i in range(size)])  33 us
    all_to_all x1, blocking collectives, shards(): got = lax.all_to_all(part, ('z', 'y'), 0, 0, tiled=True)  29.8 us
    pallas_call x2, Pallas kernels, attend(): pl.pallas_call(functools.partial(attn_kernel, blocks, first, tok, heads,...  16.6 us
    pallas_call x1, Pallas kernels, project(): pl.pallas_call(functools.partial(project_kernel, n_ctx, n_y, half), grid_...  6.97 us
    unnamed x38, local copies, waits for them, and re-layouts  5.96 us
    pallas_call x1, Pallas kernels, combine(): pl.pallas_call(functools.partial(combine_kernel, width // HD), out_shape=...  3.42 us
  transfers between devices with their start and end apart: 22, of which 10 were waited for; matrix products, arithmetic and copies ran while one was open for 5% of the time, Pallas kernels for 14%

profile of v1, /device:TPU:16, one launch (start us, length us, event | category | flops | bytes accessed | tf_op | source)
XLA Modules:
  0.0 147.0 jit_solution(3048629594941183269)
XLA Ops:
  0.0 1.5 %fusion = (bf16[256,1024]{1,0:T(8,128)(2,1)S(1)}, bf16[256,1024]{1,0:T(8,128)(2,1)S(1)}, bf16[256,1024]{1,0:T(8,128)(2,1)S(1)}) fusion(bf16[512,4096]{1,0:T(8,128)(2,1)} %param.15, s32[]{:T(128)S(6)} %select_n.24, s32[]{:T(128)S(6)} %select_n.27, s32[]{:T(128)S(6)} %select_n.25, s32[]{:T(128)S(6)} %select_n.26), kind=kLoop, calls=%fused_computation.12 | loop fusion | bytes 3145744 | tf_op jit(solution)/shard_map/weights/dynamic_slice | solution.py:249
  1.5 1.4 collective-permute-start.18
  3.8 2.5 %collective-permute-start.20 = (bf16[256,1024]{1,0:T(8,128)(2,1)S(1)}, bf16[256,1024]{1,0:T(8,128)(2,1)S(1)}, u32[]{:S(2)}, u32[]{:S(2)}) collective-permute-start(bf16[256,1024]{1,0:T(8,128)(2,1)S(1)} %get-tuple-element.15), channel_id=1, source_target_pairs={{0,6},{2,0},{4,2},{6,4},{1,7},{3,1},{5,3},{7,5},{8,14},{10,8},{12,... | collective-permute-start | bytes 1572872 | tf_op jit(solution)/shard_map/weights/ppermute | solution.py:18
  6.3 3.2 %collective-permute-start.2 = (bf16[128,512]{1,0:T(8,128)(2,1)S(1)}, bf16[128,512]{1,0:T(8,128)(2,1)S(1)}, u32[]{:S(2)}, u32[]{:S(2)}) collective-permute-start(bf16[128,512]{1,0:T(8,128)(2,1)S(1)} %copy-done.3), channel_id=1, source_target_pairs={{0,192},{64,0},{128,64},{192,128},{1,193},{65,1},{129,65},{193,129... | collective-permute-start | bytes 393224 | tf_op jit(solution)/shard_map/queries/ppermute | solution.py:18
  10.9 15.6 %collective-permute-done.18 = bf16[256,1024]{1,0:T(8,128)(2,1)S(1)} collective-permute-done((bf16[256,1024]{1,0:T(8,128)(2,1)S(1)}, bf16[256,1024]{1,0:T(8,128)(2,1)S(1)}, u32[]{:S(2)}, u32[]{:S(2)}) %collective-permute-start.18) | collective-permute-done | bytes 524320 | tf_op jit(solution)/shard_map/weights/ppermute | solution.py:18
  26.5 3.0 %collective-permute-start.1 = (bf16[128,512]{1,0:T(8,128)(2,1)S(1)}, bf16[128,512]{1,0:T(8,128)(2,1)S(1)}, u32[]{:S(2)}, u32[]{:S(2)}) collective-permute-start(bf16[128,512]{1,0:T(8,128)(2,1)S(1)} %copy-done.3), channel_id=1, source_target_pairs={{0,128},{64,192},{128,0},{192,64},{1,129},{65,193},{129,1},{193,65... | collective-permute-start | bytes 393224 | tf_op jit(solution)/shard_map/queries/ppermute | solution.py:18
  33.6 10.2 %attend.3 = (bf16[128,640]{1,0:T(8,128)(2,1)}, bf16[128,640]{1,0:T(8,128)(2,1)}, bf16[128,640]{1,0:T(8,128)(2,1)}) custom-call(s32[5]{0:T(128)} %stack.19.scalars, bf16[128,512]{1,0:T(8,128)(2,1)} %copy-done.12, bf16[128,512]{1,0:T(8,128)(2,1)} %copy-done.14, bf16[128,512]{1,0:T(8,128)(2,1)} %copy-done.13, bf16[4096,1024]{1,0:T(8,128)(2,1)} %refs_3_.3, ...), custom_call_target="tpu_custom_call" | custom-call | flops 6442450944 | bytes 2097152 | tf_op jit(solution)/shard_map/attend/attend/pallas_call | solution.py:108
  43.8 8.0 %collective-permute-start.3 = (bf16[128,640]{1,0:T(8,128)(2,1)}, bf16[128,640]{1,0:T(8,128)(2,1)S(1)}, u32[]{:S(2)}, u32[]{:S(2)}) collective-permute-start(bf16[128,640]{1,0:T(8,128)(2,1)} %get-tuple-element.10), channel_id=1, source_target_pairs={{0,192},{64,0},{128,64},{192,128},{1,193},{65,1},{129,65},{193,129... | collective-permute-start | bytes 491528 | tf_op jit(solution)/shard_map/return/ppermute | solution.py:18
  53.2 6.4 %attend.2.refs_0_ = bf16[128,640]{1,0:T(8,128)(2,1)} custom-call(s32[5]{0:T(128)} %stack.19.scalars, bf16[128,512]{1,0:T(8,128)(2,1)} %refs_0_.1, bf16[4096,1024]{1,0:T(8,128)(2,1)} %refs_3_.3, bf16[4096,1024]{1,0:T(8,128)(2,1)} %refs_4_.3, bf16[128,1024]{1,0:T(8,128)(2,1)} %refs_5_.1, bf16[128,1024]{1,0:T(8,128)(2,1)} %refs_6_.1, s32[4,128]{1,0:T(4,128)} %bitcast.14), custom_call_target="tpu_custom_call" | custom-call | flops 2147483648 | bytes 2097152 | tf_op jit(solution)/shard_map/attend/attend/pallas_call | solution.py:108
  61.3 3.4 %combine.1 = (bf16[64,512]{1,0:T(8,128)(2,1)}, bf16[64,512]{1,0:T(8,128)(2,1)}) custom-call(bf16[128,640]{1,0:T(8,128)(2,1)} %attend.2.refs_0_, bf16[128,640]{1,0:T(8,128)(2,1)} %copy-done, bf16[128,640]{1,0:T(8,128)(2,1)} %copy-done.1, bf16[128,640]{1,0:T(8,128)(2,1)} %copy-done.2), custom_call_target="tpu_custom_call" | custom-call | tf_op jit(solution)/shard_map/return/combine/pallas_call | solution.py:156
  64.7 5.2 %collective-permute-start.8 = (bf16[64,512]{1,0:T(8,128)(2,1)}, bf16[64,512]{1,0:T(8,128)(2,1)S(1)}, u32[]{:S(2)}, u32[]{:S(2)}) collective-permute-start(bf16[64,512]{1,0:T(8,128)(2,1)} %get-tuple-element.13), channel_id=1, source_target_pairs={{0,192},{64,0},{128,64},{192,128},{1,193},{65,1},{129,65},{193,129... | collective-permute-start | bytes 196616 | tf_op jit(solution)/shard_map/gather/ppermute | solution.py:18
  69.9 1.5 %collective-permute-start.7 = (bf16[64,512]{1,0:T(8,128)(2,1)}, bf16[64,512]{1,0:T(8,128)(2,1)S(1)}, u32[]{:S(2)}, u32[]{:S(2)}) collective-permute-start(bf16[64,512]{1,0:T(8,128)(2,1)} %get-tuple-element.13), channel_id=1, source_target_pairs={{0,128},{64,192},{128,0},{192,64},{1,129},{65,193},{129,1},{193,65... | collective-permute-start | bytes 196616 | tf_op jit(solution)/shard_map/gather/ppermute | solution.py:18
  73.2 2.7 %collective-permute-done.12 = bf16[64,512]{1,0:T(8,128)(2,1)S(1)} collective-permute-done((bf16[64,512]{1,0:T(8,128)(2,1)}, bf16[64,512]{1,0:T(8,128)(2,1)S(1)}, u32[]{:S(2)}, u32[]{:S(2)}) %collective-permute-start.12) | collective-permute-done | bytes 65568 | tf_op jit(solution)/shard_map/gather/ppermute | solution.py:18
  75.9 6.0 %collective-permute-done.13 = bf16[64,512]{1,0:T(8,128)(2,1)S(1)} collective-permute-done((bf16[64,512]{1,0:T(8,128)(2,1)}, bf16[64,512]{1,0:T(8,128)(2,1)S(1)}, u32[]{:S(2)}, u32[]{:S(2)}) %collective-permute-start.13) | collective-permute-done | bytes 65568 | tf_op jit(solution)/shard_map/gather/ppermute | solution.py:18
  82.1 5.0 %collective-permute-done.14 = bf16[64,512]{1,0:T(8,128)(2,1)S(1)} collective-permute-done((bf16[64,512]{1,0:T(8,128)(2,1)}, bf16[64,512]{1,0:T(8,128)(2,1)S(1)}, u32[]{:S(2)}, u32[]{:S(2)}) %collective-permute-start.14) | collective-permute-done | bytes 65568 | tf_op jit(solution)/shard_map/gather/ppermute | solution.py:18
  87.1 3.8 %collective-permute-start.17 = (bf16[256,512]{1,0:T(8,128)(2,1)S(1)}, bf16[256,512]{1,0:T(8,128)(2,1)S(1)}, u32[]{:S(2)}, u32[]{:S(2)}) collective-permute-start(bf16[256,512]{1,0:T(8,128)(2,1)S(1)} %constant_dynamic-update-slice_fusion.4.refs_4_), channel_id=1, source_target_pairs={{0,192},{64,0},{128,64},{192,128},{1,193},{65,1},{129,65},{193,129... | collective-permute-start | bytes 786440 | tf_op jit(solution)/shard_map/gather/ppermute | solution.py:18
  92.1 5.5 %collective-permute-done.17.refs_7_ = bf16[256,512]{1,0:T(8,128)(2,1)S(1)} collective-permute-done((bf16[256,512]{1,0:T(8,128)(2,1)S(1)}, bf16[256,512]{1,0:T(8,128)(2,1)S(1)}, u32[]{:S(2)}, u32[]{:S(2)}) %collective-permute-start.17) | collective-permute-done | bytes 262176 | tf_op jit(solution)/shard_map/gather/ppermute | solution.py:18
  97.6 1.3 collective-permute-done.16.refs_6_
  99.6 2.3 %constant_dynamic-slice_fusion.refs_8_ = bf16[512,1024]{1,0:T(8,128)(2,1)} fusion(bf16[512,4096]{1,0:T(8,128)(2,1)} %param.15, s32[]{:T(128)S(6)} %select_n.23), kind=kLoop, calls=%fused_computation.11 | loop fusion | bytes 2097156 | tf_op jit(solution)/shard_map/weights/dynamic_slice | solution.py:253
  101.9 3.6 %collective-permute-done.10.refs_2_ = bf16[256,512]{1,0:T(8,128)(2,1)S(1)} collective-permute-done((bf16[256,512]{1,0:T(8,128)(2,1)S(1)}, bf16[256,512]{1,0:T(8,128)(2,1)S(1)}, u32[]{:S(2)}, u32[]{:S(2)}) %collective-permute-start.10) | collective-permute-done | bytes 262176 | tf_op jit(solution)/shard_map/gather/ppermute | solution.py:18
  105.6 2.6 %collective-permute-done.9.refs_1_ = bf16[256,512]{1,0:T(8,128)(2,1)} collective-permute-done((bf16[256,512]{1,0:T(8,128)(2,1)S(1)}, bf16[256,512]{1,0:T(8,128)(2,1)}, u32[]{:S(2)}, u32[]{:S(2)}) %collective-permute-start.9) | collective-permute-done | bytes 262176 | tf_op jit(solution)/shard_map/gather/ppermute | solution.py:18
  108.2 1.2 copy-done.6
  109.4 7.0 %project.1 = bf16[512,1024]{1,0:T(8,128)(2,1)} custom-call(s32[5]{0:T(128)} %stack.19.scalars, bf16[256,512]{1,0:T(8,128)(2,1)} %copy-done.4, bf16[256,512]{1,0:T(8,128)(2,1)} %collective-permute-done.9.refs_1_, bf16[256,512]{1,0:T(8,128)(2,1)} %copy-done.11, bf16[256,512]{1,0:T(8,128)(2,1)} %copy-done.10, bf16[256,512]{1,0:T(8,128)(2,1)} %copy-done.5, ...), custom_call_target="tpu_custom_call" | custom-call | flops 2147483648 | bytes 7340032 | tf_op jit(solution)/shard_map/project/project/pallas_call | solution.py:208
  116.4 29.8 %all_to_all.9 = bf16[32,16,1024]{2,1,0:T(8,128)(2,1)S(1)} all-to-all(bf16[32,16,1024]{2,1,0:T(8,128)(2,1)} %bitcast.11), channel_id=1, replica_groups=mesh['ctx'=4,'z'=8,'y'=4,'rep'=2] {'z','y'}, dimensions={0} | all-to-all | bytes 2097152 | tf_op jit(solution)/shard_map/reduce/all_to_all | solution.py:274
  (71 shorter events, 13.4 us)
Async XLA Ops:
  1.5 25.0 %collective-permute-start.18 = (bf16[256,1024]{1,0:T(8,128)(2,1)S(1)}, bf16[256,1024]{1,0:T(8,128)(2,1)S(1)}, u32[]{:S(2)}, u32[]{:S(2)}) collective-permute-start(bf16[256,1024]{1,0:T(8,128)(2,1)S(1)} %get-tuple-element.16), channel_id=1, source_target_pairs={{0,2},{2,4},{4,6},{6,0},{1,3},{3,5},{5,7},{7,1},{8,10},{10,12},{12... | collective-permute-start | bytes 1572872 | tf_op jit(solution)/shard_map/weights/ppermute | solution.py:18
  2.9 27.5 %collective-permute-start.19 = (bf16[256,1024]{1,0:T(8,128)(2,1)S(1)}, bf16[256,1024]{1,0:T(8,128)(2,1)S(1)}, u32[]{:S(2)}, u32[]{:S(2)}) collective-permute-start(bf16[256,1024]{1,0:T(8,128)(2,1)S(1)} %get-tuple-element.17), channel_id=1, source_target_pairs={{0,4},{2,6},{4,0},{6,2},{1,5},{3,7},{5,1},{7,3},{8,12},{10,14},{12... | collective-permute-start | bytes 1572872 | tf_op jit(solution)/shard_map/weights/ppermute | solution.py:18
  3.8 27.4 %collective-permute-start.20 = (bf16[256,1024]{1,0:T(8,128)(2,1)S(1)}, bf16[256,1024]{1,0:T(8,128)(2,1)S(1)}, u32[]{:S(2)}, u32[]{:S(2)}) collective-permute-start(bf16[256,1024]{1,0:T(8,128)(2,1)S(1)} %get-tuple-element.15), channel_id=1, source_target_pairs={{0,6},{2,0},{4,2},{6,4},{1,7},{3,1},{5,3},{7,5},{8,14},{10,8},{12,... | collective-permute-start | bytes 1572872 | tf_op jit(solution)/shard_map/weights/ppermute | solution.py:18
  6.3 25.7 %collective-permute-start = (bf16[128,512]{1,0:T(8,128)(2,1)S(1)}, bf16[128,512]{1,0:T(8,128)(2,1)S(1)}, u32[]{:S(2)}, u32[]{:S(2)}) collective-permute-start(bf16[128,512]{1,0:T(8,128)(2,1)S(1)} %copy-done.3), channel_id=1, source_target_pairs={{0,64},{64,128},{128,192},{192,0},{1,65},{65,129},{129,193},{193,1... | collective-permute-start | bytes 393224 | tf_op jit(solution)/shard_map/queries/ppermute | solution.py:18
  6.3 25.7 %collective-permute-start.2 = (bf16[128,512]{1,0:T(8,128)(2,1)S(1)}, bf16[128,512]{1,0:T(8,128)(2,1)S(1)}, u32[]{:S(2)}, u32[]{:S(2)}) collective-permute-start(bf16[128,512]{1,0:T(8,128)(2,1)S(1)} %copy-done.3), channel_id=1, source_target_pairs={{0,192},{64,0},{128,64},{192,128},{1,193},{65,1},{129,65},{193,129... | collective-permute-start | bytes 393224 | tf_op jit(solution)/shard_map/queries/ppermute | solution.py:18
  26.5 6.5 %collective-permute-start.1 = (bf16[128,512]{1,0:T(8,128)(2,1)S(1)}, bf16[128,512]{1,0:T(8,128)(2,1)S(1)}, u32[]{:S(2)}, u32[]{:S(2)}) collective-permute-start(bf16[128,512]{1,0:T(8,128)(2,1)S(1)} %copy-done.3), channel_id=1, source_target_pairs={{0,128},{64,192},{128,0},{192,64},{1,129},{65,193},{129,1},{193,65... | collective-permute-start | bytes 393224 | tf_op jit(solution)/shard_map/queries/ppermute | solution.py:18
  32.0 76.1 %collective-permute-start.21 = (bf16[768,1024]{1,0:T(8,128)(2,1)}, bf16[768,1024]{1,0:T(8,128)(2,1)S(1)}, u32[]{:S(2)}, u32[]{:S(2)}) collective-permute-start(bf16[768,1024]{1,0:T(8,128)(2,1)} %constant_dynamic-update-slice_fusion.8.refs_9_), channel_id=1, source_target_pairs={{0,1},{1,0},{2,3},{3,2},{4,5},{5,4},{6,7},{7,6},{8,9},{9,8},{10,11... | collective-permute-start | bytes 4718600 | tf_op jit(solution)/shard_map/weights/ppermute | solution.py:18
  43.8 15.8 %collective-permute-start.3 = (bf16[128,640]{1,0:T(8,128)(2,1)}, bf16[128,640]{1,0:T(8,128)(2,1)S(1)}, u32[]{:S(2)}, u32[]{:S(2)}) collective-permute-start(bf16[128,640]{1,0:T(8,128)(2,1)} %get-tuple-element.10), channel_id=1, source_target_pairs={{0,192},{64,0},{128,64},{192,128},{1,193},{65,1},{129,65},{193,129... | collective-permute-start | bytes 491528 | tf_op jit(solution)/shard_map/return/ppermute | solution.py:18
  51.8 7.8 %collective-permute-start.4 = (bf16[128,640]{1,0:T(8,128)(2,1)}, bf16[128,640]{1,0:T(8,128)(2,1)S(1)}, u32[]{:S(2)}, u32[]{:S(2)}) collective-permute-start(bf16[128,640]{1,0:T(8,128)(2,1)} %get-tuple-element.11), channel_id=1, source_target_pairs={{0,128},{64,192},{128,0},{192,64},{1,129},{65,193},{129,1},{193,65... | collective-permute-start | bytes 491528 | tf_op jit(solution)/shard_map/return/ppermute | solution.py:18
  52.6 8.0 %collective-permute-start.5 = (bf16[128,640]{1,0:T(8,128)(2,1)}, bf16[128,640]{1,0:T(8,128)(2,1)S(1)}, u32[]{:S(2)}, u32[]{:S(2)}) collective-permute-start(bf16[128,640]{1,0:T(8,128)(2,1)} %get-tuple-element.12), channel_id=1, source_target_pairs={{0,64},{64,128},{128,192},{192,0},{1,65},{65,129},{129,193},{193,1... | collective-permute-start | bytes 491528 | tf_op jit(solution)/shard_map/return/ppermute | solution.py:18
  64.7 27.2 %collective-permute-start.8 = (bf16[64,512]{1,0:T(8,128)(2,1)}, bf16[64,512]{1,0:T(8,128)(2,1)S(1)}, u32[]{:S(2)}, u32[]{:S(2)}) collective-permute-start(bf16[64,512]{1,0:T(8,128)(2,1)} %get-tuple-element.13), channel_id=1, source_target_pairs={{0,192},{64,0},{128,64},{192,128},{1,193},{65,1},{129,65},{193,129... | collective-permute-start | bytes 196616 | tf_op jit(solution)/shard_map/gather/ppermute | solution.py:18
  69.9 21.3 %collective-permute-start.7 = (bf16[64,512]{1,0:T(8,128)(2,1)}, bf16[64,512]{1,0:T(8,128)(2,1)S(1)}, u32[]{:S(2)}, u32[]{:S(2)}) collective-permute-start(bf16[64,512]{1,0:T(8,128)(2,1)} %get-tuple-element.13), channel_id=1, source_target_pairs={{0,128},{64,192},{128,0},{192,64},{1,129},{65,193},{129,1},{193,65... | collective-permute-start | bytes 196616 | tf_op jit(solution)/shard_map/gather/ppermute | solution.py:18
  71.4 19.4 %collective-permute-start.6 = (bf16[64,512]{1,0:T(8,128)(2,1)}, bf16[64,512]{1,0:T(8,128)(2,1)S(1)}, u32[]{:S(2)}, u32[]{:S(2)}) collective-permute-start(bf16[64,512]{1,0:T(8,128)(2,1)} %get-tuple-element.13), channel_id=1, source_target_pairs={{0,64},{64,128},{128,192},{192,0},{1,65},{65,129},{129,193},{193,1... | collective-permute-start | bytes 196616 | tf_op jit(solution)/shard_map/gather/ppermute | solution.py:18
  71.5 4.5 %collective-permute-start.12 = (bf16[64,512]{1,0:T(8,128)(2,1)}, bf16[64,512]{1,0:T(8,128)(2,1)S(1)}, u32[]{:S(2)}, u32[]{:S(2)}) collective-permute-start(bf16[64,512]{1,0:T(8,128)(2,1)} %get-tuple-element.14), channel_id=1, source_target_pairs={{0,2},{2,4},{4,6},{6,0},{1,3},{3,5},{5,7},{7,1},{8,10},{10,12},{12... | collective-permute-start | bytes 196616 | tf_op jit(solution)/shard_map/gather/ppermute | solution.py:18
  75.9 6.0 %collective-permute-start.13 = (bf16[64,512]{1,0:T(8,128)(2,1)}, bf16[64,512]{1,0:T(8,128)(2,1)S(1)}, u32[]{:S(2)}, u32[]{:S(2)}) collective-permute-start(bf16[64,512]{1,0:T(8,128)(2,1)} %get-tuple-element.14), channel_id=1, source_target_pairs={{0,4},{2,6},{4,0},{6,2},{1,5},{3,7},{5,1},{7,3},{8,12},{10,14},{12... | collective-permute-start | bytes 196616 | tf_op jit(solution)/shard_map/gather/ppermute | solution.py:18
  81.9 5.2 %collective-permute-start.14 = (bf16[64,512]{1,0:T(8,128)(2,1)}, bf16[64,512]{1,0:T(8,128)(2,1)S(1)}, u32[]{:S(2)}, u32[]{:S(2)}) collective-permute-start(bf16[64,512]{1,0:T(8,128)(2,1)} %get-tuple-element.14), channel_id=1, source_target_pairs={{0,6},{2,0},{4,2},{6,4},{1,7},{3,1},{5,3},{7,5},{8,14},{10,8},{12,... | collective-permute-start | bytes 196616 | tf_op jit(solution)/shard_map/gather/ppermute | solution.py:18
  87.1 21.1 %copy-start.5 = (bf16[256,512]{1,0:T(8,128)(2,1)}, bf16[256,512]{1,0:T(8,128)(2,1)S(1)}, u32[]{:S(2)}) copy-start(bf16[256,512]{1,0:T(8,128)(2,1)S(1)} %constant_dynamic-update-slice_fusion.4.refs_4_) | copy-start | bytes 786436
  87.1 10.5 %collective-permute-start.17 = (bf16[256,512]{1,0:T(8,128)(2,1)S(1)}, bf16[256,512]{1,0:T(8,128)(2,1)S(1)}, u32[]{:S(2)}, u32[]{:S(2)}) collective-permute-start(bf16[256,512]{1,0:T(8,128)(2,1)S(1)} %constant_dynamic-update-slice_fusion.4.refs_4_), channel_id=1, source_target_pairs={{0,192},{64,0},{128,64},{192,128},{1,193},{65,1},{129,65},{193,129... | collective-permute-start | bytes 786440 | tf_op jit(solution)/shard_map/gather/ppermute | solution.py:18
  90.9 8.0 %collective-permute-start.16 = (bf16[256,512]{1,0:T(8,128)(2,1)S(1)}, bf16[256,512]{1,0:T(8,128)(2,1)S(1)}, u32[]{:S(2)}, u32[]{:S(2)}) collective-permute-start(bf16[256,512]{1,0:T(8,128)(2,1)S(1)} %constant_dynamic-update-slice_fusion.4.refs_4_), channel_id=1, source_target_pairs={{0,128},{64,192},{128,0},{192,64},{1,129},{65,193},{129,1},{193,65... | collective-permute-start | bytes 786440 | tf_op jit(solution)/shard_map/gather/ppermute | solution.py:18
  91.2 10.7 %collective-permute-start.15 = (bf16[256,512]{1,0:T(8,128)(2,1)S(1)}, bf16[256,512]{1,0:T(8,128)(2,1)S(1)}, u32[]{:S(2)}, u32[]{:S(2)}) collective-permute-start(bf16[256,512]{1,0:T(8,128)(2,1)S(1)} %constant_dynamic-update-slice_fusion.4.refs_4_), channel_id=1, source_target_pairs={{0,64},{64,128},{128,192},{192,0},{1,65},{65,129},{129,193},{193,1... | collective-permute-start | bytes 786440 | tf_op jit(solution)/shard_map/gather/ppermute | solution.py:18
  92.0 16.2 %copy-start.4 = (bf16[256,512]{1,0:T(8,128)(2,1)}, bf16[256,512]{1,0:T(8,128)(2,1)S(1)}, u32[]{:S(2)}) copy-start(bf16[256,512]{1,0:T(8,128)(2,1)S(1)} %constant_dynamic-update-slice_fusion.refs_0_) | copy-start | bytes 786436
  92.0 9.9 %collective-permute-start.11 = (bf16[256,512]{1,0:T(8,128)(2,1)S(1)}, bf16[256,512]{1,0:T(8,128)(2,1)S(1)}, u32[]{:S(2)}, u32[]{:S(2)}) collective-permute-start(bf16[256,512]{1,0:T(8,128)(2,1)S(1)} %constant_dynamic-update-slice_fusion.refs_0_), channel_id=1, source_target_pairs={{0,6},{2,0},{4,2},{6,4},{1,7},{3,1},{5,3},{7,5},{8,14},{10,8},{12,... | collective-permute-start | bytes 786440 | tf_op jit(solution)/shard_map/gather/ppermute | solution.py:18
  97.6 8.0 %collective-permute-start.10 = (bf16[256,512]{1,0:T(8,128)(2,1)S(1)}, bf16[256,512]{1,0:T(8,128)(2,1)S(1)}, u32[]{:S(2)}, u32[]{:S(2)}) collective-permute-start(bf16[256,512]{1,0:T(8,128)(2,1)S(1)} %constant_dynamic-update-slice_fusion.refs_0_), channel_id=1, source_target_pairs={{0,4},{2,6},{4,0},{6,2},{1,5},{3,7},{5,1},{7,3},{8,12},{10,14},{12... | collective-permute-start | bytes 786440 | tf_op jit(solution)/shard_map/gather/ppermute | solution.py:18
  98.9 9.3 %collective-permute-start.9 = (bf16[256,512]{1,0:T(8,128)(2,1)S(1)}, bf16[256,512]{1,0:T(8,128)(2,1)}, u32[]{:S(2)}, u32[]{:S(2)}) collective-permute-start(bf16[256,512]{1,0:T(8,128)(2,1)S(1)} %constant_dynamic-update-slice_fusion.refs_0_), channel_id=1, source_target_pairs={{0,2},{2,4},{4,6},{6,0},{1,3},{3,5},{5,7},{7,1},{8,10},{10,12},{12... | collective-permute-start | bytes 786440 | tf_op jit(solution)/shard_map/gather/ppermute | solution.py:18
  (13 other events, 47.7 us)

commit v2 on v0

v2 whole, which is shorter than its diff:
```python
import functools

import jax
import jax.numpy as jnp
from jax import lax
from jax.experimental import pallas as pl
from jax.experimental.pallas import tpu as pltpu
from jax.sharding import Mesh
from jax.sharding import PartitionSpec as P

HD = 128
GROUP = 16
NEG = -1e30
SCALE2 = HD**-0.5 * 1.4426950408889634
VMEM = 60 << 20
EXTRA = 16


def shift(x, axis, size, by):
    return lax.ppermute(x, axis, [(i, (i + by) % size) for i in range(size)])


def attn_kernel(blocks, begin, tok, heads, tile, chunk, n_ctx, scalars, *refs):
    q_refs = refs[:blocks]
    k_hbm, v_hbm, nk_hbm, nv_hbm, pos_ref = refs[blocks : blocks + 5]
    outs = refs[blocks + 5 : 2 * blocks + 5]
    q_s, top_s, acc_s, k_s, v_s, nk_s, nv_s, sem, new_sem = refs[2 * blocks + 5 : 2 * blocks + 14]
    buffers = refs[2 * blocks + 14 : 2 * blocks + 17], refs[2 * blocks + 17 :]
    live, kv_head, ctx = scalars[0], scalars[1], scalars[2]
    rows = tok * heads
    total = blocks * rows
    chunks = total // chunk
    steps = k_s.shape[0] // tile
    lanes = pl.ds(pl.multiple_of(kv_head * HD, HD), HD)
    tiles = (live + tile - 1) // tile
    full = live // tile

    new_copies = [
        pltpu.make_async_copy(nk_hbm.at[:, lanes], nk_s, new_sem.at[0]),
        pltpu.make_async_copy(nv_hbm.at[:, lanes], nv_s, new_sem.at[1]),
    ]

    def tile_copies(i):
        at = pl.ds(i * tile, tile)
        return [
            pltpu.make_async_copy(k_hbm.at[at, lanes], k_s.at[at, :], sem.at[0, i]),
            pltpu.make_async_copy(v_hbm.at[at, lanes], v_s.at[at, :], sem.at[1, i]),
        ]

    for copy in new_copies:
        copy.start()
    for i in range(steps):

        @pl.when(i < tiles)
        def _():
            for copy in tile_copies(i):
                copy.start()

    for b in range(blocks):
        for h in range(heads):
            q_s[pl.ds(b * rows + h * tok, tok), :] = q_refs[b][:, h * HD : (h + 1) * HD]
    for copy in new_copies:
        copy.wait()

    def score(own, keys):
        return lax.dot_general(
            q_s[own, :], keys, (((1,), (1,)), ((), ())), preferred_element_type=jnp.float32
        )

    def weigh(weights, values):
        both = jnp.concatenate([values, jnp.ones_like(values)], axis=1)
        return jnp.dot(weights.astype(jnp.bfloat16), both, preferred_element_type=jnp.float32)

    key_pos = jnp.broadcast_to(pos_ref[pl.ds(ctx, 1), :], (tok, tok))
    def start(b, carry):
        row = pos_ref[pl.ds(lax.rem(ctx + n_ctx - begin - b, n_ctx), 1), :]
        seen = key_pos <= jnp.broadcast_to(row, (tok, tok)).T
        seen = jnp.concatenate([seen] * heads, axis=0)
        own = pl.ds(pl.multiple_of(b * rows, rows), rows)
        scores = jnp.where(seen, score(own, nk_s[...]), NEG)
        top = jnp.max(scores, axis=1, keepdims=True)
        weights = jnp.where(seen, jnp.exp2((scores - top) * SCALE2), 0.0)
        acc_s[own, :] = weigh(weights, nv_s[...])
        top_s[own, :] = jnp.broadcast_to(top, (rows, HD))
        return carry

    lax.fori_loop(0, blocks, start, 0)

    def place(n):
        i = n // chunks
        c = n - i * chunks
        return (
            pl.ds(pl.multiple_of(c * chunk, chunk), chunk),
            pl.ds(pl.multiple_of(i * tile, tile), tile),
        )

    def first(n, buffer, masked=False):
        score_b, top_b, scale_b = buffer
        own, keys = place(n)
        scores = score(own, k_s[keys, :])
        if masked:
            slot = full * tile + lax.broadcasted_iota(jnp.int32, scores.shape, 1)
            scores = jnp.where(slot < live, scores, NEG)
        score_b[...] = scores
        old = top_s[own, :]
        new = jnp.maximum(old, jnp.max(scores, axis=1, keepdims=True))
        scale_b[...] = jnp.exp2((old - new) * SCALE2)
        top_b[...] = new
        top_s[own, :] = new

    def second(n, buffer):
        score_b, top_b, scale_b = buffer
        own, keys = place(n)
        weights = jnp.exp2((score_b[...] - top_b[:, :1]) * SCALE2)
        part = weigh(weights, v_s[keys, :])
        scale = scale_b[...]
        acc_s[own, :] = acc_s[own, :] * jnp.concatenate([scale, scale], axis=1) + part

    for i in range(steps):

        @pl.when(i < tiles)
        def _():
            for copy in tile_copies(i):
                copy.wait()

    def sweep(start, count, masked):
        first(start, buffers[0], masked)

        def pair(j, carry):
            n = start + 2 * j
            first(n + 1, buffers[1], masked)
            second(n, buffers[0])
            first(jnp.where(2 * j + 2 < count, n + 2, start), buffers[0], masked)
            second(n + 1, buffers[1])
            return carry

        lax.fori_loop(0, count // 2, pair, 0)

    @pl.when(full > 0)
    def _():
        sweep(0, full * chunks, False)

    @pl.when(full < tiles)
    def _():
        sweep(full * chunks, chunks, True)

    lane = lax.broadcasted_iota(jnp.int32, (tok, HD), 1)
    for b in range(blocks):
        stats = jnp.zeros((tok, HD), jnp.float32)
        for h in range(heads):
            own = pl.ds(b * rows + h * tok, tok)
            sums = acc_s[own, HD:]
            done = (acc_s[own, :HD] / sums).astype(jnp.bfloat16)
            outs[b][:tok, h * HD : (h + 1) * HD] = done
            level = top_s[own, :] * HD**-0.5 + jnp.log(sums)
            high = level.astype(jnp.bfloat16).astype(jnp.float32)
            middle = (level - high).astype(jnp.bfloat16).astype(jnp.float32)
            low = level - high - middle
            stats = jnp.where(lane == 3 * h, high, stats)
            stats = jnp.where(lane == 3 * h + 1, middle, stats)
            stats = jnp.where(lane == 3 * h + 2, low, stats)
        turned = stats.T[:EXTRA].astype(jnp.bfloat16)
        outs[b][tok:, :] = jnp.concatenate([turned] * heads, axis=1)


def attend(queries, begin, keys, values, new_keys, new_values, pos, scalars):
    blocks = len(queries)
    tok, width = queries[0].shape
    heads = width // HD
    slots = keys.shape[0]
    total = blocks * tok * heads
    tile = slots
    chunk = min(256, total // 2)
    vmem = pl.BlockSpec(memory_space=pltpu.VMEM)
    hbm = pl.BlockSpec(memory_space=pltpu.HBM)
    f32, b16 = jnp.float32, jnp.bfloat16
    buffer = [pltpu.VMEM((chunk, tile), f32)] + [pltpu.VMEM((chunk, HD), f32)] * 2
    return pl.pallas_call(
        functools.partial(attn_kernel, blocks, begin, tok, heads, tile, chunk, pos.shape[0]),
        in_specs=[pl.BlockSpec(memory_space=pltpu.SMEM)] + [vmem] * blocks + [hbm] * 4 + [vmem],
        out_specs=[vmem] * blocks,
        scratch_shapes=[
            pltpu.VMEM((total, HD), b16),
            pltpu.VMEM((total, HD), f32),
            pltpu.VMEM((total, 2 * HD), f32),
            pltpu.VMEM((slots, HD), b16),
            pltpu.VMEM((slots, HD), b16),
            pltpu.VMEM((new_keys.shape[0], HD), b16),
            pltpu.VMEM((new_keys.shape[0], HD), b16),
            pltpu.SemaphoreType.DMA((2, slots // tile)),
            pltpu.SemaphoreType.DMA((2,)),
        ]
        + buffer * 2,
        out_shape=[jax.ShapeDtypeStruct((tok + EXTRA, width), b16)] * blocks,
        compiler_params=pltpu.CompilerParams(vmem_limit_bytes=VMEM),
        cost_estimate=pl.CostEstimate(
            flops=8 * total * slots * HD, bytes_accessed=4 * slots * HD, transcendentals=total * slots
        ),
        name="attend",
    )(scalars, *queries, keys, values, new_keys, new_values, pos)


def combine_kernel(copies, spans, *refs):
    parts, out_ref = refs[:-1], refs[-1]
    tok = parts[0].shape[0] - EXTRA
    width = parts[0].shape[1]
    piece = lax.broadcasted_iota(jnp.int32, (EXTRA, width), 0)
    head = lax.broadcasted_iota(jnp.int32, (EXTRA, width), 1) // HD
    spread = ((piece >= 3 * head) & (piece < 3 * head + 3)).astype(jnp.float32).astype(jnp.bfloat16)
    levels = [
        lax.dot_general(
            p[tok:, :tok], spread, (((0,), (0,)), ((), ())), preferred_element_type=jnp.float32
        )
        for p in parts
    ]
    top = functools.reduce(jnp.maximum, levels)
    weights = [jnp.exp(level - top) for level in levels]
    total = sum(weights[1:], weights[0])
    mixed = sum(w * p[:tok, :].astype(jnp.float32) for w, p in zip(weights, parts))
    done = (mixed / total).astype(jnp.bfloat16)
    piece = tok // (2 * spans)
    for k in range(copies):
        for n in range(spans):
            at = (2 * n + k // 2 % 2) * piece
            to = (k * spans + n) * piece
            out_ref[to : to + piece, :] = done[at : at + piece]


def combine(parts, copies, spans):
    tok, width = parts[0].shape
    tok -= EXTRA
    vmem = pl.BlockSpec(memory_space=pltpu.VMEM)
    return pl.pallas_call(
        functools.partial(combine_kernel, copies, spans),
        in_specs=[vmem] * len(parts),
        out_specs=vmem,
        out_shape=jax.ShapeDtypeStruct((copies * tok // 2, width), jnp.bfloat16),
        compiler_params=pltpu.CompilerParams(vmem_limit_bytes=VMEM),
        name="combine",
    )(*parts)


def cut_kernel(scalars, weight, one_ref, two_ref, sem):
    side, core = scalars[3] % 2, scalars[4]
    cut, cols = two_ref.shape
    other = pl.ds(pl.multiple_of((1 - side) * cols, cols), cols)
    same = pl.ds(pl.multiple_of(side * cols, cols), cols)
    rows = pl.ds(pl.multiple_of(core * cut, cut), cut)
    copies = [
        pltpu.make_async_copy(weight.at[:, other], one_ref, sem.at[0]),
        pltpu.make_async_copy(weight.at[rows, same], two_ref, sem.at[1]),
    ]
    for copy in copies:
        copy.start()
    for copy in copies:
        copy.wait()


def cut_weight(weight, scalars):
    feat, cols = weight.shape
    vmem = pl.BlockSpec(memory_space=pltpu.VMEM)
    return pl.pallas_call(
        cut_kernel,
        in_specs=[
            pl.BlockSpec(memory_space=pltpu.SMEM),
            pl.BlockSpec(memory_space=pltpu.HBM),
        ],
        out_specs=[vmem, vmem],
        scratch_shapes=[pltpu.SemaphoreType.DMA((2,))],
        out_shape=[
            jax.ShapeDtypeStruct((feat, cols // 2), weight.dtype),
            jax.ShapeDtypeStruct((feat // 2, cols // 2), weight.dtype),
        ],
        compiler_params=pltpu.CompilerParams(vmem_limit_bytes=VMEM),
        cost_estimate=pl.CostEstimate(flops=0, bytes_accessed=1, transcendentals=0),
        name="cut",
    )(scalars, weight)


def mark_kernel(after, out_ref):
    out_ref[...] = jnp.zeros_like(out_ref)


def mark(after, flops):
    return pl.pallas_call(
        mark_kernel,
        in_specs=[pl.BlockSpec(memory_space=pl.ANY)],
        out_specs=pl.BlockSpec(memory_space=pltpu.VMEM),
        out_shape=jax.ShapeDtypeStruct((8, HD), jnp.float32),
        cost_estimate=pl.CostEstimate(flops=flops, bytes_accessed=0, transcendentals=0),
        name="mark",
    )(after)


def project_kernel(n_ctx, n_y, scalars, got_ref, weight, *refs):
    near, far, near_half, far_half, _, out_ref, rhs_s, acc_s, sem = refs
    y, core = scalars[3], scalars[4]
    feat, cols = near.shape
    cut = feat // 2
    lanes = pl.ds(pl.multiple_of(y % 2 * cols, cols), cols)
    one = pl.ds(pl.multiple_of(core * cut, cut), cut)
    two = pl.ds(pl.multiple_of((1 - core) * cut, cut), cut)
    first = jnp.where(core == 0, 1, 3)
    groups = [
        (y, [(weight.at[:, lanes], rhs_s.at[0])]),
        (y ^ 2, [(near_half, rhs_s.at[1, one, :]), (far_half, rhs_s.at[1, two, :])]),
        (y ^ first, [(near, rhs_s.at[2])]),
        (y ^ (4 - first), [(far, rhs_s.at[3])]),
    ]
    copies = [
        [pltpu.make_async_copy(a, b, sem.at[t, k]) for k, (a, b) in enumerate(group)]
        for t, (_, group) in enumerate(groups)
    ]
    for group in copies:
        for copy in group:
            copy.start()
    for t, (src, _) in enumerate(groups):
        lhs = jnp.concatenate([got_ref[c * n_y + src] for c in range(n_ctx)], axis=0)
        for copy in copies[t]:
            copy.wait()

        part = jnp.dot(lhs, rhs_s[t], preferred_element_type=jnp.float32)
        if t == 0:
            acc_s[...] = part
        elif t < n_y - 1:
            acc_s[...] += part
        else:
            out_ref[...] = (acc_s[...] + part).astype(out_ref.dtype)


def project(got, weight, pieces, n_ctx, n_y, scalars, after):
    blocks, tok, feat = got.shape
    cols = pieces[0].shape[1]
    rows = n_ctx * tok
    vmem = pl.BlockSpec(memory_space=pltpu.VMEM)
    hbm = pl.BlockSpec(memory_space=pltpu.HBM)
    return pl.pallas_call(
        functools.partial(project_kernel, n_ctx, n_y),
        in_specs=[pl.BlockSpec(memory_space=pltpu.SMEM), vmem] + [hbm] * (1 + len(pieces))
        + [pl.BlockSpec(memory_space=pl.ANY)],
        out_specs=vmem,
        scratch_shapes=[
            pltpu.VMEM((n_y, feat, cols), jnp.bfloat16),
            pltpu.VMEM((rows, cols), jnp.float32),
            pltpu.SemaphoreType.DMA((n_y, 2)),
        ],
        out_shape=jax.ShapeDtypeStruct((rows, cols), jnp.bfloat16),
        compiler_params=pltpu.CompilerParams(vmem_limit_bytes=VMEM),
        cost_estimate=pl.CostEstimate(
            flops=2 * rows * feat * n_y * cols, bytes_accessed=10 << 20, transcendentals=0
        ),
        name="project",
    )(scalars, got, weight, *pieces, after)


def shards(
    sizes,
    queries,
    history_keys,
    history_values,
    new_keys,
    new_values,
    shard_lengths,
    positions,
    out_weight,
):
    n_ctx, n_z, n_y, n_rep = sizes
    ctx, z, core = (lax.axis_index(a) for a in ("ctx", "z", "rep"))
    side = lax.axis_index("side")
    y = 2 * lax.axis_index("pair") + side
    kv_head = (z * n_y + y) * (queries.shape[1] // HD) // GROUP
    scalars = jnp.stack([shard_lengths[0], kv_head, ctx, y, core]).astype(jnp.int32)
    pos = positions.reshape(n_ctx, -1)

    feat, all_cols = out_weight.shape
    cols = all_cols // 2
    cut = feat // n_rep
    history = (history_keys, history_values, new_keys, new_values, pos, scalars)

    with jax.named_scope("queries"):
        others = [shift(queries, "ctx", n_ctx, s) for s in range(1, n_ctx)]
    axes = ("pair", "side", "rep")
    devices = [(i, r) for i in range(n_y) for r in range(n_rep)]

    def send(block, flips):
        pairs = [(i * n_rep + r, (i ^ flips[r]) * n_rep + r) for i, r in devices]
        return lax.ppermute(block, axes, pairs)

    with jax.named_scope("weights"):
        one, two = cut_weight(out_weight, scalars)
        near = send(one, (1, 3))
        passing = send(two, (1, 3))
    with jax.named_scope("attend"):
        sent = attend(others, 1, *history)
        sent, passing = lax.optimization_barrier((sent, passing))
    with jax.named_scope("return"):
        back = [shift(p, "ctx", n_ctx, -s) for s, p in enumerate(sent, 1)]
    with jax.named_scope("weights"):
        near_half = send(passing, (3, 1))
    with jax.named_scope("attend"):
        mine, _ = lax.optimization_barrier((queries, sent))
        (kept,) = attend([mine], 0, *history)
    with jax.named_scope("combine"):
        own = combine([kept] + back, n_ctx * n_y, n_z // n_ctx)
        _, near, near_half = lax.optimization_barrier((own, near, near_half))
    with jax.named_scope("gather"):
        got = lax.all_to_all(own, ("ctx", "pair", "side"), 0, 0, tiled=True)
        got = got.reshape(n_ctx * n_y, -1, feat)
    with jax.named_scope("weights"):
        far = shift(near, "rep", n_rep, 1)
        far_half = shift(near_half, "rep", n_rep, 1)
    with jax.named_scope("project"):
        pieces = (near, far, near_half, far_half)
        part = project(got, out_weight, pieces, n_ctx, n_y, scalars, mark(got, 80 << 30))
    with jax.named_scope("reduce"):
        got = lax.all_to_all(part, ("z", "side"), 0, 0, tiled=True)
        got = got.reshape(n_z, 2, -1, cols).astype(jnp.float32)
        mixed = jnp.sum(got, axis=0).astype(jnp.bfloat16)
        return mixed.transpose(1, 0, 2).reshape(-1, all_cols)


def solution(mesh):
    n_ctx, n_head, n_rep = (mesh.shape[a] for a in ("ctx", "head", "rep"))
    n_y = n_ctx
    n_z = n_head // n_y
    devices = mesh.devices.reshape(n_ctx, n_z, n_y // 2, 2, n_rep)
    fine = Mesh(devices, ("ctx", "z", "pair", "side", "rep"))
    head = ("z", "pair", "side")
    in_specs = (
        P(("rep", "ctx"), head),
        P(("rep", "ctx"), None),
        P(("rep", "ctx"), None),
        P(("rep", "ctx"), None),
        P(("rep", "ctx"), None),
        P(("rep", "ctx")),
        P("rep"),
        P(head, "ctx"),
    )
    return jax.shard_map(
        functools.partial(shards, (n_ctx, n_z, n_y, n_rep)),
        mesh=fine,
        in_specs=in_specs,
        out_specs=P(("rep", *head), "ctx"),
        check_vma=False,
    )
```

time: 396 us -> 115 us (0.29)
  waiting for transfers between devices: 243 us -> 17.4 us
  matrix products: 53.3 us -> 0 us
  Pallas kernels: 0 us -> 34.8 us
  local copies, waits for them, and re-layouts: 26 us -> 4.17 us
  other arithmetic: 21.7 us -> 0.15 us
  between operations: 13.6 us -> 0.82 us
  starting transfers between devices: 10.1 us -> 21.1 us
  blocking collectives: 26.4 us -> 36.1 us
    reduce_scatter x1 -> x0, waiting for transfers between devices: 230 us -> none  [shards(): lax.psum_scatter(partial_sum, 'head', scatter_dimension=0, tiled=True)]
    dot_general x19 -> x0, matrix products: 53.3 us -> none  [the longest x9 39.2 us: add_block(): jnp.einsum('qgjk,kgd->qgjd', weights, value_tile, preferred_element_type=...]
    all_to_all x0 -> x1, blocking collectives: none -> 36.1 us  [shards(): got = lax.all_to_all(part, ('z', 'side'), 0, 0, tiled=True)]
    pallas_call x0 -> x6, Pallas kernels: none -> 34.8 us  [the longest x2 20.8 us: attend(): pl.pallas_call(functools.partial(attn_kernel, blocks, begin, tok, heads,...]
    all_gather x2 -> x0, blocking collectives: 26.4 us -> none  [the longest x1 14.4 us: shards(): gathered = lax.all_gather(queries, 'ctx', axis=0, tiled=True)]
    while x24 -> x0, local copies, waits for them, and re-layouts: 15.4 us -> none
    ppermute x0 -> x11, starting transfers between devices: none -> 13.5 us  [the longest x8 10.9 us: shift(): return lax.ppermute(x, axis, [(i, (i + by) % size) for i in range(size)])]
    reduce_sum x11 -> x1, other arithmetic: 10.3 us -> 0.15 us  [shards(): mixed = jnp.sum(got, axis=0).astype(jnp.bfloat16)]
  transfers between devices with their start and end apart: 4 -> 12, of which waited for: 4 -> 4; matrix products, arithmetic and copies ran while one was open for 2% -> 0% of each run, Pallas kernels for 0% -> 21%
where the time goes in v2:
time: 115 us
  blocking collectives  36.1 us (31%)
  Pallas kernels  34.8 us (30%)
  starting transfers between devices  21.1 us (18%)
  waiting for transfers between devices  17.4 us (15%)
  local copies, waits for them, and re-layouts  4.17 us (4%)
    all_to_all x1, blocking collectives, shards(): got = lax.all_to_all(part, ('z', 'side'), 0, 0, tiled=True)  36.1 us
    pallas_call x2, Pallas kernels, attend(): pl.pallas_call(functools.partial(attn_kernel, blocks, begin, tok, heads,...  20.8 us
    all_to_all x1, waiting for transfers between devices, shards(): got = lax.all_to_all(own, ('ctx', 'pair', 'side'), 0, 0, tiled=True)  13.9 us
    ppermute x8, starting transfers between devices, shift(): return lax.ppermute(x, axis, [(i, (i + by) % size) for i in range(size)])  10.9 us
    all_to_all x1, starting transfers between devices, shards(): got = lax.all_to_all(own, ('ctx', 'pair', 'side'), 0, 0, tiled=True)  7.62 us
    pallas_call x1, Pallas kernels, project(): pl.pallas_call(functools.partial(project_kernel, n_ctx, n_y), in_specs=[p...  6.56 us
    pallas_call x1, Pallas kernels, cut_weight(): pl.pallas_call(cut_kernel, in_specs=[pl.BlockSpec(memory_space=pltpu.SMEM...  4.18 us
    ppermute x8, waiting for transfers between devices, shift(): return lax.ppermute(x, axis, [(i, (i + by) % size) for i in range(size)])  3.52 us
  transfers between devices with their start and end apart: 12, of which 4 were waited for; matrix products, arithmetic and copies ran while one was open for 0% of the time, Pallas kernels for 21%

profile of v2, /device:TPU:16, one launch (start us, length us, event | category | flops | bytes accessed | tf_op | source)
XLA Modules:
  0.0 114.6 jit_solution(13675167231899218839)
XLA Ops:
  0.7 0.7 stack.19.scalars
  1.4 4.2 %cut.1 = (bf16[512,2048]{1,0:T(8,128)(2,1)}, bf16[256,2048]{1,0:T(8,128)(2,1)}) custom-call(s32[5]{0:T(128)} %stack.19.scalars, bf16[512,4096]{1,0:T(8,128)(2,1)} %weight.3), custom_call_target="tpu_custom_call" | custom-call | bytes 1 | tf_op jit(solution)/shard_map/weights/cut/pallas_call | solution.py:262
  5.6 1.4 %collective-permute-start.3 = (bf16[256,2048]{1,0:T(8,128)(2,1)}, bf16[256,2048]{1,0:T(8,128)(2,1)}, u32[]{:S(2)}, u32[]{:S(2)}) collective-permute-start(bf16[256,2048]{1,0:T(8,128)(2,1)} %get-tuple-element.20), channel_id=1, source_target_pairs={{0,2},{1,7},{2,0},{3,5},{4,6},{5,3},{6,4},{7,1},{8,10},{9,15},{10,... | collective-permute-start | bytes 3145736 | tf_op jit(solution)/shard_map/weights/ppermute | solution.py:387
  6.9 0.7 collective-permute-start.7
  7.7 3.0 %collective-permute-start.1 = (bf16[128,512]{1,0:T(8,128)(2,1)S(1)}, bf16[128,512]{1,0:T(8,128)(2,1)S(1)}, u32[]{:S(2)}, u32[]{:S(2)}) collective-permute-start(bf16[128,512]{1,0:T(8,128)(2,1)S(1)} %copy-done.5), channel_id=1, source_target_pairs={{0,128},{64,192},{128,0},{192,64},{1,129},{65,193},{129,1},{193,65... | collective-permute-start | bytes 393224 | tf_op jit(solution)/shard_map/queries/ppermute | solution.py:20
  10.7 0.6 collective-permute-start
  11.3 2.6 %collective-permute-start.2 = (bf16[128,512]{1,0:T(8,128)(2,1)S(1)}, bf16[128,512]{1,0:T(8,128)(2,1)S(1)}, u32[]{:S(2)}, u32[]{:S(2)}) collective-permute-start(bf16[128,512]{1,0:T(8,128)(2,1)S(1)} %copy-done.5), channel_id=1, source_target_pairs={{0,192},{64,0},{128,64},{192,128},{1,193},{65,1},{129,65},{193,129... | collective-permute-start | bytes 393224 | tf_op jit(solution)/shard_map/queries/ppermute | solution.py:20
  13.9 1.5 %collective-permute-done.1.refs_1_ = bf16[128,512]{1,0:T(8,128)(2,1)S(1)} collective-permute-done((bf16[128,512]{1,0:T(8,128)(2,1)S(1)}, bf16[128,512]{1,0:T(8,128)(2,1)S(1)}, u32[]{:S(2)}, u32[]{:S(2)}) %collective-permute-start.1) | collective-permute-done | bytes 131104 | tf_op jit(solution)/shard_map/queries/ppermute | solution.py:20
  15.4 1.8 %collective-permute-done.refs_0_ = bf16[128,512]{1,0:T(8,128)(2,1)S(1)} collective-permute-done((bf16[128,512]{1,0:T(8,128)(2,1)S(1)}, bf16[128,512]{1,0:T(8,128)(2,1)S(1)}, u32[]{:S(2)}, u32[]{:S(2)}) %collective-permute-start) | collective-permute-done | bytes 131104 | tf_op jit(solution)/shard_map/queries/ppermute | solution.py:20
  17.3 0.6 copy-done.7
  18.0 13.6 %attend.2 = (bf16[144,512]{1,0:T(8,128)(2,1)}, bf16[144,512]{1,0:T(8,128)(2,1)}, bf16[144,512]{1,0:T(8,128)(2,1)}) custom-call(s32[5]{0:T(128)} %stack.19.scalars, bf16[128,512]{1,0:T(8,128)(2,1)} %copy-done.7, bf16[128,512]{1,0:T(8,128)(2,1)} %copy-done.6, bf16[128,512]{1,0:T(8,128)(2,1)} %copy-done.8, bf16[4096,1024]{1,0:T(8,128)(2,1)} %refs_1_.1, ...), custom_call_target="tpu_custom_call" | custom-call | flops 6442450944 | bytes 2097152 | tf_op jit(solution)/shard_map/attend/attend/pallas_call | solution.py:178
  31.5 2.9 %collective-permute-start.4 = (bf16[144,512]{1,0:T(8,128)(2,1)}, bf16[144,512]{1,0:T(8,128)(2,1)S(1)}, u32[]{:S(2)}, u32[]{:S(2)}) collective-permute-start(bf16[144,512]{1,0:T(8,128)(2,1)} %get-tuple-element.21), channel_id=1, source_target_pairs={{0,192},{64,0},{128,64},{192,128},{1,193},{65,1},{129,65},{193,129... | collective-permute-start | bytes 442376 | tf_op jit(solution)/shard_map/return/ppermute | solution.py:20
  34.6 1.0 collective-permute-start.6
  36.1 7.2 %attend.3.refs_0_ = bf16[144,512]{1,0:T(8,128)(2,1)} custom-call(s32[5]{0:T(128)} %stack.19.scalars, bf16[128,512]{1,0:T(8,128)(2,1)} %refs_0_, bf16[4096,1024]{1,0:T(8,128)(2,1)} %refs_1_.1, bf16[4096,1024]{1,0:T(8,128)(2,1)} %refs_2_.1, bf16[128,1024]{1,0:T(8,128)(2,1)} %refs_3_.3, bf16[128,1024]{1,0:T(8,128)(2,1)} %refs_4_.3, s32[4,128]{1,0:T(4,128)} %bitcast.16), custom_call_target="tpu_custom_call" | custom-call | flops 2147483648 | bytes 2097152 | tf_op jit(solution)/shard_map/attend/attend/pallas_call | solution.py:178
  44.0 0.6 copy-done.4
  44.7 2.7 %combine.1 = bf16[1024,512]{1,0:T(8,128)(2,1)} custom-call(bf16[144,512]{1,0:T(8,128)(2,1)} %attend.3.refs_0_, bf16[144,512]{1,0:T(8,128)(2,1)} %copy-done.2, bf16[144,512]{1,0:T(8,128)(2,1)} %copy-done.3, bf16[144,512]{1,0:T(8,128)(2,1)} %copy-done.4), custom_call_target="tpu_custom_call" | custom-call | tf_op jit(solution)/shard_map/combine/combine/pallas_call | solution.py:233
  47.3 7.6 %all-to-all-start = ((bf16[16,64,512]{2,1,0:T(8,128)(2,1)}), bf16[16,64,512]{2,1,0:T(8,128)(2,1)S(1)}, u32[]{:S(2)}, u32[]{:S(2)}) async-start(bf16[16,64,512]{2,1,0:T(8,128)(2,1)} %bitcast.12), calls=%async_computation | async-start | bytes 2097152 | tf_op jit(solution)/shard_map/gather/all_to_all | solution.py:407
  55.1 0.5 collective-permute-start.9
  55.6 13.9 %all-to-all-done.after.got_ref = bf16[16,64,512]{2,1,0:T(8,128)(2,1)S(1)} async-done(((bf16[16,64,512]{2,1,0:T(8,128)(2,1)}), bf16[16,64,512]{2,1,0:T(8,128)(2,1)S(1)}, u32[]{:S(2)}, u32[]{:S(2)}) %all-to-all-start) | async-done | bytes 1048608 | tf_op jit(solution)/shard_map/gather/all_to_all | solution.py:407
  69.5 1.0 copy-done
  70.4 0.6 mark.1.refs_4_
  71.0 6.6 %project.1 = bf16[256,2048]{1,0:T(8,128)(2,1)} custom-call(s32[5]{0:T(128)} %stack.19.scalars, bf16[16,64,512]{2,1,0:T(8,128)(2,1)} %copy-done, bf16[512,4096]{1,0:T(8,128)(2,1)} %weight.3, bf16[512,2048]{1,0:T(8,128)(2,1)} %copy-done.1, bf16[512,2048]{1,0:T(8,128)(2,1)} %collective-permute-done.9.refs_1_, bf16[256,2048]{1,0:T(8,128)(2,1)} %collective-permute-done.8.refs_2_, ...), custom_call_target="tpu_custom_call" | custom-call | flops 2147483648 | bytes 10485760 | tf_op jit(solution)/shard_map/project/project/pallas_call | solution.py:337
  77.6 36.1 %all_to_all.18 = bf16[16,16,2048]{2,1,0:T(8,128)(2,1)S(1)} all-to-all(bf16[16,16,2048]{2,1,0:T(8,128)(2,1)} %bitcast.11), channel_id=1, replica_groups=mesh['ctx'=4,'z'=8,'pair'=2,'side'=2,'rep'=2] {'z','side'}, dimensions={0} | all-to-all | bytes 2097152 | tf_op jit(solution)/shard_map/reduce/all_to_all | solution.py:416
  113.9 0.7 copy.10
  (28 shorter events, 1.6 us)
Async XLA Ops:
  0.0 7.7 %copy-start.5 = (bf16[128,512]{1,0:T(8,128)(2,1)S(1)}, bf16[128,512]{1,0:T(8,128)(2,1)}, u32[]{:S(2)}) copy-start(bf16[128,512]{1,0:T(8,128)(2,1)} %refs_0_) | copy-start | bytes 393220
  5.6 26.0 %collective-permute-start.3 = (bf16[256,2048]{1,0:T(8,128)(2,1)}, bf16[256,2048]{1,0:T(8,128)(2,1)}, u32[]{:S(2)}, u32[]{:S(2)}) collective-permute-start(bf16[256,2048]{1,0:T(8,128)(2,1)} %get-tuple-element.20), channel_id=1, source_target_pairs={{0,2},{1,7},{2,0},{3,5},{4,6},{5,3},{6,4},{7,1},{8,10},{9,15},{10,... | collective-permute-start | bytes 3145736 | tf_op jit(solution)/shard_map/weights/ppermute | solution.py:387
  6.9 48.0 %collective-permute-start.7 = (bf16[512,2048]{1,0:T(8,128)(2,1)}, bf16[512,2048]{1,0:T(8,128)(2,1)S(1)}, u32[]{:S(2)}, u32[]{:S(2)}) collective-permute-start(bf16[512,2048]{1,0:T(8,128)(2,1)} %get-tuple-element.25), channel_id=1, source_target_pairs={{0,2},{1,7},{2,0},{3,5},{4,6},{5,3},{6,4},{7,1},{8,10},{9,15},{10,... | collective-permute-start | bytes 6291464 | tf_op jit(solution)/shard_map/weights/ppermute | solution.py:387
  7.7 7.8 %collective-permute-start.1 = (bf16[128,512]{1,0:T(8,128)(2,1)S(1)}, bf16[128,512]{1,0:T(8,128)(2,1)S(1)}, u32[]{:S(2)}, u32[]{:S(2)}) collective-permute-start(bf16[128,512]{1,0:T(8,128)(2,1)S(1)} %copy-done.5), channel_id=1, source_target_pairs={{0,128},{64,192},{128,0},{192,64},{1,129},{65,193},{129,1},{193,65... | collective-permute-start | bytes 393224 | tf_op jit(solution)/shard_map/queries/ppermute | solution.py:20
  10.7 6.6 %collective-permute-start = (bf16[128,512]{1,0:T(8,128)(2,1)S(1)}, bf16[128,512]{1,0:T(8,128)(2,1)S(1)}, u32[]{:S(2)}, u32[]{:S(2)}) collective-permute-start(bf16[128,512]{1,0:T(8,128)(2,1)S(1)} %copy-done.5), channel_id=1, source_target_pairs={{0,64},{64,128},{128,192},{192,0},{1,65},{65,129},{129,193},{193,1... | collective-permute-start | bytes 393224 | tf_op jit(solution)/shard_map/queries/ppermute | solution.py:20
  11.3 6.0 %collective-permute-start.2 = (bf16[128,512]{1,0:T(8,128)(2,1)S(1)}, bf16[128,512]{1,0:T(8,128)(2,1)S(1)}, u32[]{:S(2)}, u32[]{:S(2)}) collective-permute-start(bf16[128,512]{1,0:T(8,128)(2,1)S(1)} %copy-done.5), channel_id=1, source_target_pairs={{0,192},{64,0},{128,64},{192,128},{1,193},{65,1},{129,65},{193,129... | collective-permute-start | bytes 393224 | tf_op jit(solution)/shard_map/queries/ppermute | solution.py:20
  15.4 1.9 %copy-start.6 = (bf16[128,512]{1,0:T(8,128)(2,1)}, bf16[128,512]{1,0:T(8,128)(2,1)S(1)}, u32[]{:S(2)}) copy-start(bf16[128,512]{1,0:T(8,128)(2,1)S(1)} %collective-permute-done.1.refs_1_) | copy-start | bytes 393220
  17.3 0.7 copy-start.7
  17.3 0.7 copy-start.8
  31.5 11.8 %collective-permute-start.4 = (bf16[144,512]{1,0:T(8,128)(2,1)}, bf16[144,512]{1,0:T(8,128)(2,1)S(1)}, u32[]{:S(2)}, u32[]{:S(2)}) collective-permute-start(bf16[144,512]{1,0:T(8,128)(2,1)} %get-tuple-element.21), channel_id=1, source_target_pairs={{0,192},{64,0},{128,64},{192,128},{1,193},{65,1},{129,65},{193,129... | collective-permute-start | bytes 442376 | tf_op jit(solution)/shard_map/return/ppermute | solution.py:20
  34.5 8.8 %collective-permute-start.5 = (bf16[144,512]{1,0:T(8,128)(2,1)}, bf16[144,512]{1,0:T(8,128)(2,1)S(1)}, u32[]{:S(2)}, u32[]{:S(2)}) collective-permute-start(bf16[144,512]{1,0:T(8,128)(2,1)} %get-tuple-element.22), channel_id=1, source_target_pairs={{0,128},{64,192},{128,0},{192,64},{1,129},{65,193},{129,1},{193,65... | collective-permute-start | bytes 442376 | tf_op jit(solution)/shard_map/return/ppermute | solution.py:20
  34.6 8.9 %collective-permute-start.6 = (bf16[144,512]{1,0:T(8,128)(2,1)}, bf16[144,512]{1,0:T(8,128)(2,1)S(1)}, u32[]{:S(2)}, u32[]{:S(2)}) collective-permute-start(bf16[144,512]{1,0:T(8,128)(2,1)} %get-tuple-element.23), channel_id=1, source_target_pairs={{0,64},{64,128},{128,192},{192,0},{1,65},{65,129},{129,193},{193,1... | collective-permute-start | bytes 442376 | tf_op jit(solution)/shard_map/return/ppermute | solution.py:20
  35.6 19.3 %collective-permute-start.8 = (bf16[256,2048]{1,0:T(8,128)(2,1)}, bf16[256,2048]{1,0:T(8,128)(2,1)}, u32[]{:S(2)}, u32[]{:S(2)}) collective-permute-start(bf16[256,2048]{1,0:T(8,128)(2,1)} %collective-permute-done.3), channel_id=1, source_target_pairs={{0,6},{1,3},{2,4},{3,1},{4,2},{5,7},{6,0},{7,5},{8,14},{9,11},{10,... | collective-permute-start | bytes 3145736 | tf_op jit(solution)/shard_map/weights/ppermute | solution.py:387
  43.3 0.6 copy-start.2
  43.3 0.7 copy-start.3
  44.0 0.7 copy-start.4
  47.3 22.1 %all-to-all-start = ((bf16[16,64,512]{2,1,0:T(8,128)(2,1)}), bf16[16,64,512]{2,1,0:T(8,128)(2,1)S(1)}, u32[]{:S(2)}, u32[]{:S(2)}) async-start(bf16[16,64,512]{2,1,0:T(8,128)(2,1)} %bitcast.12), calls=%async_computation | async-start | bytes 2097152 | tf_op jit(solution)/shard_map/gather/all_to_all | solution.py:407
  55.0 16.1 %copy-start.1 = (bf16[512,2048]{1,0:T(8,128)(2,1)}, bf16[512,2048]{1,0:T(8,128)(2,1)S(1)}, u32[]{:S(2)}) copy-start(bf16[512,2048]{1,0:T(8,128)(2,1)S(1)} %collective-permute-done.7.refs_0_) | copy-start | bytes 6291460
  55.0 16.1 %collective-permute-start.10 = (bf16[256,2048]{1,0:T(8,128)(2,1)}, bf16[256,2048]{1,0:T(8,128)(2,1)}, u32[]{:S(2)}, u32[]{:S(2)}) collective-permute-start(bf16[256,2048]{1,0:T(8,128)(2,1)} %collective-permute-done.8.refs_2_), channel_id=1, source_target_pairs={{0,1},{1,0},{2,3},{3,2},{4,5},{5,4},{6,7},{7,6},{8,9},{9,8},{10,11... | collective-permute-start | bytes 3145736 | tf_op jit(solution)/shard_map/weights/ppermute | solution.py:20
  55.1 16.0 %collective-permute-start.9 = (bf16[512,2048]{1,0:T(8,128)(2,1)S(1)}, bf16[512,2048]{1,0:T(8,128)(2,1)}, u32[]{:S(2)}, u32[]{:S(2)}) collective-permute-start(bf16[512,2048]{1,0:T(8,128)(2,1)S(1)} %collective-permute-done.7.refs_0_), channel_id=1, source_target_pairs={{0,1},{1,0},{2,3},{3,2},{4,5},{5,4},{6,7},{7,6},{8,9},{9,8},{10,11... | collective-permute-start | bytes 6291464 | tf_op jit(solution)/shard_map/weights/ppermute | solution.py:20
  69.5 1.0 copy-start

commit v3 on v2

--- a/solution.py
+++ b/solution.py
@@ -12,7 +12,7 @@
 GROUP = 16
 NEG = -1e30
 SCALE2 = HD**-0.5 * 1.4426950408889634
-VMEM = 60 << 20
+VMEM = 57 << 20
 EXTRA = 16
 
 
@@ -235,7 +235,7 @@
         in_specs=[vmem] * len(parts),
         out_specs=vmem,
         out_shape=jax.ShapeDtypeStruct((copies * tok // 2, width), jnp.bfloat16),
-        compiler_params=pltpu.CompilerParams(vmem_limit_bytes=VMEM),
+        compiler_params=pltpu.CompilerParams(vmem_limit_bytes=VMEM // 2),
         name="combine",
     )(*parts)
 
@@ -287,6 +287,7 @@
         in_specs=[pl.BlockSpec(memory_space=pl.ANY)],
         out_specs=pl.BlockSpec(memory_space=pltpu.VMEM),
         out_shape=jax.ShapeDtypeStruct((8, HD), jnp.float32),
+        compiler_params=pltpu.CompilerParams(vmem_limit_bytes=1 << 20),
         cost_estimate=pl.CostEstimate(flops=flops, bytes_accessed=0, transcendentals=0),
         name="mark",
     )(after)

time: 115 us -> 114 us (level)
  Pallas kernels: 34.8 us -> 32.6 us
    unnamed x18 -> x16, local copies, waits for them, and re-layouts: 2.84 us -> 3.17 us
  transfers between devices with their start and end apart: 12 -> 12, of which waited for: 4 -> 4; matrix products, arithmetic and copies ran while one was open for 0% -> 0% of each run, Pallas kernels for 21% -> 19%
where the time goes in v3:
time: 114 us
  blocking collectives  36.7 us (32%)
  Pallas kernels  32.6 us (29%)
  starting transfers between devices  21.3 us (19%)
  waiting for transfers between devices  18 us (16%)
  local copies, waits for them, and re-layouts  4.5 us (4%)
    all_to_all x1, blocking collectives, shards(): got = lax.all_to_all(part, ('z', 'side'), 0, 0, tiled=True)  36.7 us
    pallas_call x2, Pallas kernels, attend(): pl.pallas_call(functools.partial(attn_kernel, blocks, begin, tok, heads,...  20.3 us
    all_to_all x1, waiting for transfers between devices, shards(): got = lax.all_to_all(own, ('ctx', 'pair', 'side'), 0, 0, tiled=True)  14 us
    ppermute x8, starting transfers between devices, shift(): return lax.ppermute(x, axis, [(i, (i + by) % size) for i in range(size)])  11.3 us
    all_to_all x1, starting transfers between devices, shards(): got = lax.all_to_all(own, ('ctx', 'pair', 'side'), 0, 0, tiled=True)  7.44 us
    pallas_call x1, Pallas kernels, project(): pl.pallas_call(functools.partial(project_kernel, n_ctx, n_y), in_specs=[p...  6.54 us
    pallas_call x1, Pallas kernels, cut_weight(): pl.pallas_call(cut_kernel, in_specs=[pl.BlockSpec(memory_space=pltpu.SMEM...  4.21 us
    ppermute x8, waiting for transfers between devices, shift(): return lax.ppermute(x, axis, [(i, (i + by) % size) for i in range(size)])  3.95 us
  transfers between devices with their start and end apart: 12, of which 4 were waited for; matrix products, arithmetic and copies ran while one was open for 0% of the time, Pallas kernels for 19%

profile of v3, /device:TPU:16, one launch (start us, length us, event | category | flops | bytes accessed | tf_op | source)
XLA Modules:
  0.0 114.1 jit_solution(5519132671071457368)
XLA Ops:
  0.7 0.7 stack.19.scalars
  1.4 4.2 %cut.1 = (bf16[512,2048]{1,0:T(8,128)(2,1)}, bf16[256,2048]{1,0:T(8,128)(2,1)}) custom-call(s32[5]{0:T(128)} %stack.19.scalars, bf16[512,4096]{1,0:T(8,128)(2,1)} %weight.3), custom_call_target="tpu_custom_call" | custom-call | bytes 1 | tf_op jit(solution)/shard_map/weights/cut/pallas_call | solution.py:262
  5.6 1.4 %collective-permute-start.3 = (bf16[256,2048]{1,0:T(8,128)(2,1)}, bf16[256,2048]{1,0:T(8,128)(2,1)}, u32[]{:S(2)}, u32[]{:S(2)}) collective-permute-start(bf16[256,2048]{1,0:T(8,128)(2,1)} %get-tuple-element.20), channel_id=1, source_target_pairs={{0,2},{1,7},{2,0},{3,5},{4,6},{5,3},{6,4},{7,1},{8,10},{9,15},{10,... | collective-permute-start | bytes 3145736 | tf_op jit(solution)/shard_map/weights/ppermute | solution.py:388
  6.9 0.7 collective-permute-start.7
  7.7 3.0 %collective-permute-start.1 = (bf16[128,512]{1,0:T(8,128)(2,1)S(1)}, bf16[128,512]{1,0:T(8,128)(2,1)S(1)}, u32[]{:S(2)}, u32[]{:S(2)}) collective-permute-start(bf16[128,512]{1,0:T(8,128)(2,1)S(1)} %copy-done.4), channel_id=1, source_target_pairs={{0,128},{64,192},{128,0},{192,64},{1,129},{65,193},{129,1},{193,65... | collective-permute-start | bytes 393224 | tf_op jit(solution)/shard_map/queries/ppermute | solution.py:20
  10.7 0.6 collective-permute-start
  11.3 2.6 %collective-permute-start.2 = (bf16[128,512]{1,0:T(8,128)(2,1)S(1)}, bf16[128,512]{1,0:T(8,128)(2,1)S(1)}, u32[]{:S(2)}, u32[]{:S(2)}) collective-permute-start(bf16[128,512]{1,0:T(8,128)(2,1)S(1)} %copy-done.4), channel_id=1, source_target_pairs={{0,192},{64,0},{128,64},{192,128},{1,193},{65,1},{129,65},{193,129... | collective-permute-start | bytes 393224 | tf_op jit(solution)/shard_map/queries/ppermute | solution.py:20
  14.0 1.5 %collective-permute-done.1.refs_1_ = bf16[128,512]{1,0:T(8,128)(2,1)S(1)} collective-permute-done((bf16[128,512]{1,0:T(8,128)(2,1)S(1)}, bf16[128,512]{1,0:T(8,128)(2,1)S(1)}, u32[]{:S(2)}, u32[]{:S(2)}) %collective-permute-start.1) | collective-permute-done | bytes 131104 | tf_op jit(solution)/shard_map/queries/ppermute | solution.py:20
  15.4 1.8 %collective-permute-done.refs_0_ = bf16[128,512]{1,0:T(8,128)(2,1)S(1)} collective-permute-done((bf16[128,512]{1,0:T(8,128)(2,1)S(1)}, bf16[128,512]{1,0:T(8,128)(2,1)S(1)}, u32[]{:S(2)}, u32[]{:S(2)}) %collective-permute-start) | collective-permute-done | bytes 131104 | tf_op jit(solution)/shard_map/queries/ppermute | solution.py:20
  17.3 0.6 copy-done.6
  18.0 13.5 %attend.2 = (bf16[144,512]{1,0:T(8,128)(2,1)}, bf16[144,512]{1,0:T(8,128)(2,1)}, bf16[144,512]{1,0:T(8,128)(2,1)}) custom-call(s32[5]{0:T(128)} %stack.19.scalars, bf16[128,512]{1,0:T(8,128)(2,1)} %copy-done.6, bf16[128,512]{1,0:T(8,128)(2,1)} %copy-done.5, bf16[128,512]{1,0:T(8,128)(2,1)} %copy-done.7, bf16[4096,1024]{1,0:T(8,128)(2,1)} %refs_1_.1, ...), custom_call_target="tpu_custom_call" | custom-call | flops 6442450944 | bytes 2097152 | tf_op jit(solution)/shard_map/attend/attend/pallas_call | solution.py:178
  31.5 3.0 %collective-permute-start.4 = (bf16[144,512]{1,0:T(8,128)(2,1)}, bf16[144,512]{1,0:T(8,128)(2,1)S(1)}, u32[]{:S(2)}, u32[]{:S(2)}) collective-permute-start(bf16[144,512]{1,0:T(8,128)(2,1)} %get-tuple-element.21), channel_id=1, source_target_pairs={{0,192},{64,0},{128,64},{192,128},{1,193},{65,1},{129,65},{193,129... | collective-permute-start | bytes 442376 | tf_op jit(solution)/shard_map/return/ppermute | solution.py:20
  34.7 1.0 collective-permute-start.6
  36.1 6.8 %attend.3.refs_0_ = bf16[144,512]{1,0:T(8,128)(2,1)} custom-call(s32[5]{0:T(128)} %stack.19.scalars, bf16[128,512]{1,0:T(8,128)(2,1)} %refs_0_, bf16[4096,1024]{1,0:T(8,128)(2,1)} %refs_1_.1, bf16[4096,1024]{1,0:T(8,128)(2,1)} %refs_2_.1, bf16[128,1024]{1,0:T(8,128)(2,1)} %refs_3_.3, bf16[128,1024]{1,0:T(8,128)(2,1)} %refs_4_.3, s32[4,128]{1,0:T(4,128)} %bitcast.15), custom_call_target="tpu_custom_call" | custom-call | flops 2147483648 | bytes 2097152 | tf_op jit(solution)/shard_map/attend/attend/pallas_call | solution.py:178
  43.0 0.6 collective-permute-done.6.refs_3_
  43.6 0.9 copy-done.1
  44.5 1.5 %combine.1 = bf16[1024,512]{1,0:T(8,128)(2,1)} custom-call(bf16[144,512]{1,0:T(8,128)(2,1)S(1)} %copy-done.1, bf16[144,512]{1,0:T(8,128)(2,1)S(1)} %collective-permute-done.4.refs_1_, bf16[144,512]{1,0:T(8,128)(2,1)S(1)} %collective-permute-done.5.refs_2_, bf16[144,512]{1,0:T(8,128)(2,1)S(1)} %collective-permute-done.6.refs_3_), custom_call_target="tpu_custom_call" | custom-call | tf_op jit(solution)/shard_map/combine/combine/pallas_call | solution.py:233
  46.0 7.4 %all-to-all-start = ((bf16[16,64,512]{2,1,0:T(8,128)(2,1)}), bf16[16,64,512]{2,1,0:T(8,128)(2,1)S(1)}, u32[]{:S(2)}, u32[]{:S(2)}) async-start(bf16[16,64,512]{2,1,0:T(8,128)(2,1)} %bitcast.5), calls=%async_computation | async-start | bytes 2097152 | tf_op jit(solution)/shard_map/gather/all_to_all | solution.py:408
  53.5 0.8 collective-permute-start.10
  54.4 14.0 %all-to-all-done.after.got_ref = bf16[16,64,512]{2,1,0:T(8,128)(2,1)S(1)} async-done(((bf16[16,64,512]{2,1,0:T(8,128)(2,1)}), bf16[16,64,512]{2,1,0:T(8,128)(2,1)S(1)}, u32[]{:S(2)}, u32[]{:S(2)}) %all-to-all-start) | async-done | bytes 1048608 | tf_op jit(solution)/shard_map/gather/all_to_all | solution.py:408
  68.5 1.0 copy-done
  70.0 6.5 %project.1 = bf16[256,2048]{1,0:T(8,128)(2,1)} custom-call(s32[5]{0:T(128)} %stack.19.scalars, bf16[16,64,512]{2,1,0:T(8,128)(2,1)} %copy-done, bf16[512,4096]{1,0:T(8,128)(2,1)} %weight.3, bf16[512,2048]{1,0:T(8,128)(2,1)} %copy-done.3, bf16[512,2048]{1,0:T(8,128)(2,1)} %collective-permute-done.9.refs_1_, bf16[256,2048]{1,0:T(8,128)(2,1)} %collective-permute-done.8.refs_2_, ...), custom_call_target="tpu_custom_call" | custom-call | flops 2147483648 | bytes 10485760 | tf_op jit(solution)/shard_map/project/project/pallas_call | solution.py:338
  76.6 36.7 %all_to_all.18 = bf16[16,16,2048]{2,1,0:T(8,128)(2,1)S(1)} all-to-all(bf16[16,16,2048]{2,1,0:T(8,128)(2,1)} %bitcast.11), channel_id=1, replica_groups=mesh['ctx'=4,'z'=8,'pair'=2,'side'=2,'rep'=2] {'z','side'}, dimensions={0} | all-to-all | bytes 2097152 | tf_op jit(solution)/shard_map/reduce/all_to_all | solution.py:417
  113.4 0.7 copy.10
  (26 shorter events, 1.5 us)
Async XLA Ops:
  0.0 7.7 %copy-start.4 = (bf16[128,512]{1,0:T(8,128)(2,1)S(1)}, bf16[128,512]{1,0:T(8,128)(2,1)}, u32[]{:S(2)}) copy-start(bf16[128,512]{1,0:T(8,128)(2,1)} %refs_0_) | copy-start | bytes 393220
  5.6 25.9 %collective-permute-start.3 = (bf16[256,2048]{1,0:T(8,128)(2,1)}, bf16[256,2048]{1,0:T(8,128)(2,1)}, u32[]{:S(2)}, u32[]{:S(2)}) collective-permute-start(bf16[256,2048]{1,0:T(8,128)(2,1)} %get-tuple-element.20), channel_id=1, source_target_pairs={{0,2},{1,7},{2,0},{3,5},{4,6},{5,3},{6,4},{7,1},{8,10},{9,15},{10,... | collective-permute-start | bytes 3145736 | tf_op jit(solution)/shard_map/weights/ppermute | solution.py:388
  6.9 46.5 %collective-permute-start.7 = (bf16[512,2048]{1,0:T(8,128)(2,1)}, bf16[512,2048]{1,0:T(8,128)(2,1)S(1)}, u32[]{:S(2)}, u32[]{:S(2)}) collective-permute-start(bf16[512,2048]{1,0:T(8,128)(2,1)} %get-tuple-element.25), channel_id=1, source_target_pairs={{0,2},{1,7},{2,0},{3,5},{4,6},{5,3},{6,4},{7,1},{8,10},{9,15},{10,... | collective-permute-start | bytes 6291464 | tf_op jit(solution)/shard_map/weights/ppermute | solution.py:388
  7.7 7.8 %collective-permute-start.1 = (bf16[128,512]{1,0:T(8,128)(2,1)S(1)}, bf16[128,512]{1,0:T(8,128)(2,1)S(1)}, u32[]{:S(2)}, u32[]{:S(2)}) collective-permute-start(bf16[128,512]{1,0:T(8,128)(2,1)S(1)} %copy-done.4), channel_id=1, source_target_pairs={{0,128},{64,192},{128,0},{192,64},{1,129},{65,193},{129,1},{193,65... | collective-permute-start | bytes 393224 | tf_op jit(solution)/shard_map/queries/ppermute | solution.py:20
  10.7 6.6 %collective-permute-start = (bf16[128,512]{1,0:T(8,128)(2,1)S(1)}, bf16[128,512]{1,0:T(8,128)(2,1)S(1)}, u32[]{:S(2)}, u32[]{:S(2)}) collective-permute-start(bf16[128,512]{1,0:T(8,128)(2,1)S(1)} %copy-done.4), channel_id=1, source_target_pairs={{0,64},{64,128},{128,192},{192,0},{1,65},{65,129},{129,193},{193,1... | collective-permute-start | bytes 393224 | tf_op jit(solution)/shard_map/queries/ppermute | solution.py:20
  11.3 6.0 %collective-permute-start.2 = (bf16[128,512]{1,0:T(8,128)(2,1)S(1)}, bf16[128,512]{1,0:T(8,128)(2,1)S(1)}, u32[]{:S(2)}, u32[]{:S(2)}) collective-permute-start(bf16[128,512]{1,0:T(8,128)(2,1)S(1)} %copy-done.4), channel_id=1, source_target_pairs={{0,192},{64,0},{128,64},{192,128},{1,193},{65,1},{129,65},{193,129... | collective-permute-start | bytes 393224 | tf_op jit(solution)/shard_map/queries/ppermute | solution.py:20
  15.4 1.9 %copy-start.5 = (bf16[128,512]{1,0:T(8,128)(2,1)}, bf16[128,512]{1,0:T(8,128)(2,1)S(1)}, u32[]{:S(2)}) copy-start(bf16[128,512]{1,0:T(8,128)(2,1)S(1)} %collective-permute-done.1.refs_1_) | copy-start | bytes 393220
  17.3 0.7 copy-start.6
  17.3 0.7 copy-start.7
  31.5 11.4 %collective-permute-start.4 = (bf16[144,512]{1,0:T(8,128)(2,1)}, bf16[144,512]{1,0:T(8,128)(2,1)S(1)}, u32[]{:S(2)}, u32[]{:S(2)}) collective-permute-start(bf16[144,512]{1,0:T(8,128)(2,1)} %get-tuple-element.21), channel_id=1, source_target_pairs={{0,192},{64,0},{128,64},{192,128},{1,193},{65,1},{129,65},{193,129... | collective-permute-start | bytes 442376 | tf_op jit(solution)/shard_map/return/ppermute | solution.py:20
  34.5 8.4 %collective-permute-start.5 = (bf16[144,512]{1,0:T(8,128)(2,1)}, bf16[144,512]{1,0:T(8,128)(2,1)S(1)}, u32[]{:S(2)}, u32[]{:S(2)}) collective-permute-start(bf16[144,512]{1,0:T(8,128)(2,1)} %get-tuple-element.22), channel_id=1, source_target_pairs={{0,128},{64,192},{128,0},{192,64},{1,129},{65,193},{129,1},{193,65... | collective-permute-start | bytes 442376 | tf_op jit(solution)/shard_map/return/ppermute | solution.py:20
  34.7 8.9 %collective-permute-start.6 = (bf16[144,512]{1,0:T(8,128)(2,1)}, bf16[144,512]{1,0:T(8,128)(2,1)S(1)}, u32[]{:S(2)}, u32[]{:S(2)}) collective-permute-start(bf16[144,512]{1,0:T(8,128)(2,1)} %get-tuple-element.23), channel_id=1, source_target_pairs={{0,64},{64,128},{128,192},{192,0},{1,65},{65,129},{129,193},{193,1... | collective-permute-start | bytes 442376 | tf_op jit(solution)/shard_map/return/ppermute | solution.py:20
  35.6 17.8 %collective-permute-start.8 = (bf16[256,2048]{1,0:T(8,128)(2,1)}, bf16[256,2048]{1,0:T(8,128)(2,1)}, u32[]{:S(2)}, u32[]{:S(2)}) collective-permute-start(bf16[256,2048]{1,0:T(8,128)(2,1)} %collective-permute-done.3), channel_id=1, source_target_pairs={{0,6},{1,3},{2,4},{3,1},{4,2},{5,7},{6,0},{7,5},{8,14},{9,11},{10,... | collective-permute-start | bytes 3145736 | tf_op jit(solution)/shard_map/weights/ppermute | solution.py:388
  43.6 0.9 copy-start.1
  46.0 22.4 %all-to-all-start = ((bf16[16,64,512]{2,1,0:T(8,128)(2,1)}), bf16[16,64,512]{2,1,0:T(8,128)(2,1)S(1)}, u32[]{:S(2)}, u32[]{:S(2)}) async-start(bf16[16,64,512]{2,1,0:T(8,128)(2,1)} %bitcast.5), calls=%async_computation | async-start | bytes 2097152 | tf_op jit(solution)/shard_map/gather/all_to_all | solution.py:408
  53.5 15.0 %copy-start.3 = (bf16[512,2048]{1,0:T(8,128)(2,1)}, bf16[512,2048]{1,0:T(8,128)(2,1)S(1)}, u32[]{:S(2)}) copy-start(bf16[512,2048]{1,0:T(8,128)(2,1)S(1)} %collective-permute-done.7.refs_0_) | copy-start | bytes 6291460
  53.5 16.5 %collective-permute-start.10 = (bf16[256,2048]{1,0:T(8,128)(2,1)}, bf16[256,2048]{1,0:T(8,128)(2,1)}, u32[]{:S(2)}, u32[]{:S(2)}) collective-permute-start(bf16[256,2048]{1,0:T(8,128)(2,1)} %collective-permute-done.8.refs_2_), channel_id=1, source_target_pairs={{0,1},{1,0},{2,3},{3,2},{4,5},{5,4},{6,7},{7,6},{8,9},{9,8},{10,11... | collective-permute-start | bytes 3145736 | tf_op jit(solution)/shard_map/weights/ppermute | solution.py:20
  54.3 15.7 %collective-permute-start.9 = (bf16[512,2048]{1,0:T(8,128)(2,1)S(1)}, bf16[512,2048]{1,0:T(8,128)(2,1)}, u32[]{:S(2)}, u32[]{:S(2)}) collective-permute-start(bf16[512,2048]{1,0:T(8,128)(2,1)S(1)} %collective-permute-done.7.refs_0_), channel_id=1, source_target_pairs={{0,1},{1,0},{2,3},{3,2},{4,5},{5,4},{6,7},{7,6},{8,9},{9,8},{10,11... | collective-permute-start | bytes 6291464 | tf_op jit(solution)/shard_map/weights/ppermute | solution.py:20
  68.4 1.0 copy-start
  69.4 0.6 copy-start.2

commit v4 on v3

--- a/solution.py
+++ b/solution.py
@@ -240,43 +240,6 @@
     )(*parts)
 
 
-def cut_kernel(scalars, weight, one_ref, two_ref, sem):
-    side, core = scalars[3] % 2, scalars[4]
-    cut, cols = two_ref.shape
-    other = pl.ds(pl.multiple_of((1 - side) * cols, cols), cols)
-    same = pl.ds(pl.multiple_of(side * cols, cols), cols)
-    rows = pl.ds(pl.multiple_of(core * cut, cut), cut)
-    copies = [
-        pltpu.make_async_copy(weight.at[:, other], one_ref, sem.at[0]),
-        pltpu.make_async_copy(weight.at[rows, same], two_ref, sem.at[1]),
-    ]
-    for copy in copies:
-        copy.start()
-    for copy in copies:
-        copy.wait()
-
-
-def cut_weight(weight, scalars):
-    feat, cols = weight.shape
-    vmem = pl.BlockSpec(memory_space=pltpu.VMEM)
-    return pl.pallas_call(
-        cut_kernel,
-        in_specs=[
-            pl.BlockSpec(memory_space=pltpu.SMEM),
-            pl.BlockSpec(memory_space=pltpu.HBM),
-        ],
-        out_specs=[vmem, vmem],
-        scratch_shapes=[pltpu.SemaphoreType.DMA((2,))],
-        out_shape=[
-            jax.ShapeDtypeStruct((feat, cols // 2), weight.dtype),
-            jax.ShapeDtypeStruct((feat // 2, cols // 2), weight.dtype),
-        ],
-        compiler_params=pltpu.CompilerParams(vmem_limit_bytes=VMEM),
-        cost_estimate=pl.CostEstimate(flops=0, bytes_accessed=1, transcendentals=0),
-        name="cut",
-    )(scalars, weight)
-
-
 def mark_kernel(after, out_ref):
     out_ref[...] = jnp.zeros_like(out_ref)
 
@@ -388,7 +351,8 @@
         return lax.ppermute(block, axes, pairs)
 
     with jax.named_scope("weights"):
-        one, two = cut_weight(out_weight, scalars)
+        one = lax.dynamic_slice(out_weight, (0, (1 - side) * cols), (feat, cols))
+        two = lax.dynamic_slice(out_weight, (core * cut, side * cols), (cut, cols))
         near = send(one, (1, 3))
         passing = send(two, (1, 3))
     with jax.named_scope("attend"):

time: 114 us -> 112 us (0.982)
  local copies, waits for them, and re-layouts: 4.5 us -> 8.75 us
  Pallas kernels: 32.6 us -> 28.9 us
  waiting for transfers between devices: 18 us -> 16.5 us
    pallas_call x1 -> x0, Pallas kernels: 4.21 us -> none  [cut_weight(): pl.pallas_call(cut_kernel, in_specs=[pl.BlockSpec(memory_space=pltpu.SMEM...]
    dynamic_slice x0 -> x2, local copies, waits for them, and re-layouts: none -> 3.05 us  [the longest x1 1.73 us: shards(): one = lax.dynamic_slice(out_weight, (0, (1 - side) * cols), (feat, cols))]
    ppermute x8, waiting for transfers between devices: 3.95 us -> 2.35 us  [shift(): return lax.ppermute(x, axis, [(i, (i + by) % size) for i in range(size)])]
    unnamed x16 -> x14, local copies, waits for them, and re-layouts: 3.17 us -> 4.45 us
  transfers between devices with their start and end apart: 12 -> 12, of which waited for: 4 -> 4; matrix products, arithmetic and copies ran while one was open for 0% -> 2% of each run, Pallas kernels for 19% -> 20%
where the time goes in v4:
time: 112 us; the launch traced here: 113 us
  blocking collectives  36.6 us (33%)
  Pallas kernels  28.9 us (26%)
  starting transfers between devices  21 us (19%)
  waiting for transfers between devices  16.5 us (15%)
  local copies, waits for them, and re-layouts  8.75 us (8%)
    all_to_all x1, blocking collectives, shards(): got = lax.all_to_all(part, ('z', 'side'), 0, 0, tiled=True)  36.6 us
    pallas_call x2, Pallas kernels, attend(): pl.pallas_call(functools.partial(attn_kernel, blocks, begin, tok, heads,...  20.8 us
    all_to_all x1, waiting for transfers between devices, shards(): got = lax.all_to_all(own, ('ctx', 'pair', 'side'), 0, 0, tiled=True)  14.1 us
    ppermute x8, starting transfers between devices, shift(): return lax.ppermute(x, axis, [(i, (i + by) % size) for i in range(size)])  10.4 us
    all_to_all x1, starting transfers between devices, shards(): got = lax.all_to_all(own, ('ctx', 'pair', 'side'), 0, 0, tiled=True)  7.9 us
    pallas_call x1, Pallas kernels, project(): pl.pallas_call(functools.partial(project_kernel, n_ctx, n_y), in_specs=[p...  6.53 us
    unnamed x14, local copies, waits for them, and re-layouts  4.45 us
    ppermute x3, starting transfers between devices, send(): return lax.ppermute(block, axes, pairs)  2.65 us
  transfers between devices with their start and end apart: 12, of which 4 were waited for; matrix products, arithmetic and copies ran while one was open for 2% of the time, Pallas kernels for 20%

profile of v4, /device:TPU:16, one launch (start us, length us, event | category | flops | bytes accessed | tf_op | source)
XLA Modules:
  0.0 112.6 jit_solution(8855692316654571113)
XLA Ops:
  0.0 1.3 %dynamic_slice.6 = bf16[256,2048]{1,0:T(8,128)(2,1)S(1)} dynamic-slice(bf16[512,4096]{1,0:T(8,128)(2,1)} %weight.1, s32[]{:T(128)S(6)} %select_n.15, s32[]{:T(128)S(6)} %select_n.16), dynamic_slice_sizes={256,2048} | dynamic-slice | bytes 2097156 | tf_op jit(solution)/shard_map/weights/dynamic_slice | solution.py:355
  1.3 1.4 %collective-permute-start.3 = (bf16[256,2048]{1,0:T(8,128)(2,1)S(1)}, bf16[256,2048]{1,0:T(8,128)(2,1)}, u32[]{:S(2)}, u32[]{:S(2)}) collective-permute-start(bf16[256,2048]{1,0:T(8,128)(2,1)S(1)} %dynamic_slice.6), channel_id=1, source_target_pairs={{0,2},{1,7},{2,0},{3,5},{4,6},{5,3},{6,4},{7,1},{8,10},{9,15},{10,... | collective-permute-start | bytes 3145736 | tf_op jit(solution)/shard_map/weights/ppermute | solution.py:351
  2.7 1.7 %constant_dynamic-slice_fusion = bf16[512,2048]{1,0:T(8,128)(2,1)S(1)} fusion(bf16[512,4096]{1,0:T(8,128)(2,1)} %weight.1, s32[]{:T(128)S(6)} %select_n.17), kind=kLoop, calls=%fused_computation | loop fusion | bytes 4194308 | tf_op jit(solution)/shard_map/weights/dynamic_slice | solution.py:354
  4.4 0.8 collective-permute-start.7
  5.3 3.0 %collective-permute-start.1 = (bf16[128,512]{1,0:T(8,128)(2,1)S(1)}, bf16[128,512]{1,0:T(8,128)(2,1)S(1)}, u32[]{:S(2)}, u32[]{:S(2)}) collective-permute-start(bf16[128,512]{1,0:T(8,128)(2,1)S(1)} %copy-done.4), channel_id=1, source_target_pairs={{0,128},{64,192},{128,0},{192,64},{1,129},{65,193},{129,1},{193,65... | collective-permute-start | bytes 393224 | tf_op jit(solution)/shard_map/queries/ppermute | solution.py:20
  8.3 0.6 collective-permute-start
  8.9 2.6 %collective-permute-start.2 = (bf16[128,512]{1,0:T(8,128)(2,1)S(1)}, bf16[128,512]{1,0:T(8,128)(2,1)}, u32[]{:S(2)}, u32[]{:S(2)}) collective-permute-start(bf16[128,512]{1,0:T(8,128)(2,1)S(1)} %copy-done.4), channel_id=1, source_target_pairs={{0,192},{64,0},{128,64},{192,128},{1,193},{65,1},{129,65},{193,129... | collective-permute-start | bytes 393224 | tf_op jit(solution)/shard_map/queries/ppermute | solution.py:20
  12.2 0.6 stack.19.scalars
  13.0 1.8 %collective-permute-done.refs_0_ = bf16[128,512]{1,0:T(8,128)(2,1)S(1)} collective-permute-done((bf16[128,512]{1,0:T(8,128)(2,1)S(1)}, bf16[128,512]{1,0:T(8,128)(2,1)S(1)}, u32[]{:S(2)}, u32[]{:S(2)}) %collective-permute-start) | collective-permute-done | bytes 131104 | tf_op jit(solution)/shard_map/queries/ppermute | solution.py:20
  14.9 0.6 copy-done.6
  15.5 13.6 %attend.2 = (bf16[144,512]{1,0:T(8,128)(2,1)}, bf16[144,512]{1,0:T(8,128)(2,1)}, bf16[144,512]{1,0:T(8,128)(2,1)}) custom-call(s32[5]{0:T(128)} %stack.19.scalars, bf16[128,512]{1,0:T(8,128)(2,1)} %copy-done.6, bf16[128,512]{1,0:T(8,128)(2,1)} %copy-done.5, bf16[128,512]{1,0:T(8,128)(2,1)} %collective-permute-done.2.refs_2_, bf16[4096,1024]{1,0:T(8,128)(2,1)} %refs_1_.1, ...), custom_call_target="tpu_custom_call" | custom-call | flops 6442450944 | bytes 2097152 | tf_op jit(solution)/shard_map/attend/attend/pallas_call | solution.py:178
  29.1 2.4 %collective-permute-start.4 = (bf16[144,512]{1,0:T(8,128)(2,1)}, bf16[144,512]{1,0:T(8,128)(2,1)S(1)}, u32[]{:S(2)}, u32[]{:S(2)}) collective-permute-start(bf16[144,512]{1,0:T(8,128)(2,1)} %get-tuple-element.18), channel_id=1, source_target_pairs={{0,192},{64,0},{128,64},{192,128},{1,193},{65,1},{129,65},{193,129... | collective-permute-start | bytes 442376 | tf_op jit(solution)/shard_map/return/ppermute | solution.py:20
  31.6 0.6 collective-permute-start.5
  33.1 7.2 %attend.3.refs_0_ = bf16[144,512]{1,0:T(8,128)(2,1)} custom-call(s32[5]{0:T(128)} %stack.19.scalars, bf16[128,512]{1,0:T(8,128)(2,1)} %refs_0_, bf16[4096,1024]{1,0:T(8,128)(2,1)} %refs_1_.1, bf16[4096,1024]{1,0:T(8,128)(2,1)} %refs_2_.1, bf16[128,1024]{1,0:T(8,128)(2,1)} %refs_3_.3, bf16[128,1024]{1,0:T(8,128)(2,1)} %refs_4_.3, s32[4,128]{1,0:T(4,128)} %bitcast.15), custom_call_target="tpu_custom_call" | custom-call | flops 2147483648 | bytes 2097152 | tf_op jit(solution)/shard_map/attend/attend/pallas_call | solution.py:178
  40.6 0.9 copy-done.1
  41.5 1.6 %combine.1 = bf16[1024,512]{1,0:T(8,128)(2,1)} custom-call(bf16[144,512]{1,0:T(8,128)(2,1)S(1)} %copy-done.1, bf16[144,512]{1,0:T(8,128)(2,1)S(1)} %collective-permute-done.4.refs_1_, bf16[144,512]{1,0:T(8,128)(2,1)S(1)} %collective-permute-done.5.refs_2_, bf16[144,512]{1,0:T(8,128)(2,1)S(1)} %collective-permute-done.6.refs_3_), custom_call_target="tpu_custom_call" | custom-call | tf_op jit(solution)/shard_map/combine/combine/pallas_call | solution.py:233
  43.1 7.9 %all-to-all-start = ((bf16[16,64,512]{2,1,0:T(8,128)(2,1)}), bf16[16,64,512]{2,1,0:T(8,128)(2,1)S(1)}, u32[]{:S(2)}, u32[]{:S(2)}) async-start(bf16[16,64,512]{2,1,0:T(8,128)(2,1)} %bitcast.5), calls=%async_computation | async-start | bytes 2097152 | tf_op jit(solution)/shard_map/gather/all_to_all | solution.py:372
  51.6 14.1 %all-to-all-done.after.got_ref = bf16[16,64,512]{2,1,0:T(8,128)(2,1)S(1)} async-done(((bf16[16,64,512]{2,1,0:T(8,128)(2,1)}), bf16[16,64,512]{2,1,0:T(8,128)(2,1)S(1)}, u32[]{:S(2)}, u32[]{:S(2)}) %all-to-all-start) | async-done | bytes 1048608 | tf_op jit(solution)/shard_map/gather/all_to_all | solution.py:372
  65.7 1.0 copy-done
  66.7 0.6 copy-done.2
  67.3 1.3 %copy-done.3 = bf16[512,2048]{1,0:T(8,128)(2,1)} copy-done((bf16[512,2048]{1,0:T(8,128)(2,1)}, bf16[512,2048]{1,0:T(8,128)(2,1)S(1)}, u32[]{:S(2)}) %copy-start.3) | copy-done | bytes 2097176
  68.6 6.5 %project.1 = bf16[256,2048]{1,0:T(8,128)(2,1)} custom-call(s32[5]{0:T(128)} %stack.19.scalars, bf16[16,64,512]{2,1,0:T(8,128)(2,1)} %copy-done, bf16[512,4096]{1,0:T(8,128)(2,1)} %weight.1, bf16[512,2048]{1,0:T(8,128)(2,1)} %collective-permute-done.7.refs_0_, bf16[512,2048]{1,0:T(8,128)(2,1)} %copy-done.3, bf16[256,2048]{1,0:T(8,128)(2,1)} %collective-permute-done.8.refs_2_, ...), custom_call_target="tpu_custom_call" | custom-call | flops 2147483648 | bytes 10485760 | tf_op jit(solution)/shard_map/project/project/pallas_call | solution.py:301
  75.2 36.6 %all_to_all.18 = bf16[16,16,2048]{2,1,0:T(8,128)(2,1)S(1)} all-to-all(bf16[16,16,2048]{2,1,0:T(8,128)(2,1)} %bitcast.11), channel_id=1, replica_groups=mesh['ctx'=4,'z'=8,'pair'=2,'side'=2,'rep'=2] {'z','side'}, dimensions={0} | all-to-all | bytes 2097152 | tf_op jit(solution)/shard_map/reduce/all_to_all | solution.py:381
  111.9 0.7 copy.10
  (25 shorter events, 2.2 us)
Async XLA Ops:
  0.0 5.3 %copy-start.4 = (bf16[128,512]{1,0:T(8,128)(2,1)S(1)}, bf16[128,512]{1,0:T(8,128)(2,1)}, u32[]{:S(2)}) copy-start(bf16[128,512]{1,0:T(8,128)(2,1)} %refs_0_) | copy-start | bytes 393220
  1.3 27.8 %collective-permute-start.3 = (bf16[256,2048]{1,0:T(8,128)(2,1)S(1)}, bf16[256,2048]{1,0:T(8,128)(2,1)}, u32[]{:S(2)}, u32[]{:S(2)}) collective-permute-start(bf16[256,2048]{1,0:T(8,128)(2,1)S(1)} %dynamic_slice.6), channel_id=1, source_target_pairs={{0,2},{1,7},{2,0},{3,5},{4,6},{5,3},{6,4},{7,1},{8,10},{9,15},{10,... | collective-permute-start | bytes 3145736 | tf_op jit(solution)/shard_map/weights/ppermute | solution.py:351
  4.4 46.6 %collective-permute-start.7 = (bf16[512,2048]{1,0:T(8,128)(2,1)S(1)}, bf16[512,2048]{1,0:T(8,128)(2,1)}, u32[]{:S(2)}, u32[]{:S(2)}) collective-permute-start(bf16[512,2048]{1,0:T(8,128)(2,1)S(1)} %constant_dynamic-slice_fusion), channel_id=1, source_target_pairs={{0,2},{1,7},{2,0},{3,5},{4,6},{5,3},{6,4},{7,1},{8,10},{9,15},{10,... | collective-permute-start | bytes 6291464 | tf_op jit(solution)/shard_map/weights/ppermute | solution.py:351
  5.3 7.8 %collective-permute-start.1 = (bf16[128,512]{1,0:T(8,128)(2,1)S(1)}, bf16[128,512]{1,0:T(8,128)(2,1)S(1)}, u32[]{:S(2)}, u32[]{:S(2)}) collective-permute-start(bf16[128,512]{1,0:T(8,128)(2,1)S(1)} %copy-done.4), channel_id=1, source_target_pairs={{0,128},{64,192},{128,0},{192,64},{1,129},{65,193},{129,1},{193,65... | collective-permute-start | bytes 393224 | tf_op jit(solution)/shard_map/queries/ppermute | solution.py:20
  8.3 6.6 %collective-permute-start = (bf16[128,512]{1,0:T(8,128)(2,1)S(1)}, bf16[128,512]{1,0:T(8,128)(2,1)S(1)}, u32[]{:S(2)}, u32[]{:S(2)}) collective-permute-start(bf16[128,512]{1,0:T(8,128)(2,1)S(1)} %copy-done.4), channel_id=1, source_target_pairs={{0,64},{64,128},{128,192},{192,0},{1,65},{65,129},{129,193},{193,1... | collective-permute-start | bytes 393224 | tf_op jit(solution)/shard_map/queries/ppermute | solution.py:20
  8.9 6.0 %collective-permute-start.2 = (bf16[128,512]{1,0:T(8,128)(2,1)S(1)}, bf16[128,512]{1,0:T(8,128)(2,1)}, u32[]{:S(2)}, u32[]{:S(2)}) collective-permute-start(bf16[128,512]{1,0:T(8,128)(2,1)S(1)} %copy-done.4), channel_id=1, source_target_pairs={{0,192},{64,0},{128,64},{192,128},{1,193},{65,1},{129,65},{193,129... | collective-permute-start | bytes 393224 | tf_op jit(solution)/shard_map/queries/ppermute | solution.py:20
  13.0 1.9 %copy-start.5 = (bf16[128,512]{1,0:T(8,128)(2,1)}, bf16[128,512]{1,0:T(8,128)(2,1)S(1)}, u32[]{:S(2)}) copy-start(bf16[128,512]{1,0:T(8,128)(2,1)S(1)} %collective-permute-done.1.refs_1_) | copy-start | bytes 393220
  14.9 0.7 copy-start.6
  29.1 11.3 %collective-permute-start.4 = (bf16[144,512]{1,0:T(8,128)(2,1)}, bf16[144,512]{1,0:T(8,128)(2,1)S(1)}, u32[]{:S(2)}, u32[]{:S(2)}) collective-permute-start(bf16[144,512]{1,0:T(8,128)(2,1)} %get-tuple-element.18), channel_id=1, source_target_pairs={{0,192},{64,0},{128,64},{192,128},{1,193},{65,1},{129,65},{193,129... | collective-permute-start | bytes 442376 | tf_op jit(solution)/shard_map/return/ppermute | solution.py:20
  31.6 8.8 %collective-permute-start.5 = (bf16[144,512]{1,0:T(8,128)(2,1)}, bf16[144,512]{1,0:T(8,128)(2,1)S(1)}, u32[]{:S(2)}, u32[]{:S(2)}) collective-permute-start(bf16[144,512]{1,0:T(8,128)(2,1)} %get-tuple-element.19), channel_id=1, source_target_pairs={{0,128},{64,192},{128,0},{192,64},{1,129},{65,193},{129,1},{193,65... | collective-permute-start | bytes 442376 | tf_op jit(solution)/shard_map/return/ppermute | solution.py:20
  32.2 8.4 %collective-permute-start.6 = (bf16[144,512]{1,0:T(8,128)(2,1)}, bf16[144,512]{1,0:T(8,128)(2,1)S(1)}, u32[]{:S(2)}, u32[]{:S(2)}) collective-permute-start(bf16[144,512]{1,0:T(8,128)(2,1)} %get-tuple-element.20), channel_id=1, source_target_pairs={{0,64},{64,128},{128,192},{192,0},{1,65},{65,129},{129,193},{193,1... | collective-permute-start | bytes 442376 | tf_op jit(solution)/shard_map/return/ppermute | solution.py:20
  32.7 18.3 %collective-permute-start.8 = (bf16[256,2048]{1,0:T(8,128)(2,1)}, bf16[256,2048]{1,0:T(8,128)(2,1)}, u32[]{:S(2)}, u32[]{:S(2)}) collective-permute-start(bf16[256,2048]{1,0:T(8,128)(2,1)} %collective-permute-done.3), channel_id=1, source_target_pairs={{0,6},{1,3},{2,4},{3,1},{4,2},{5,7},{6,0},{7,5},{8,14},{9,11},{10,... | collective-permute-start | bytes 3145736 | tf_op jit(solution)/shard_map/weights/ppermute | solution.py:351
  40.6 0.9 copy-start.1
  43.1 22.6 %all-to-all-start = ((bf16[16,64,512]{2,1,0:T(8,128)(2,1)}), bf16[16,64,512]{2,1,0:T(8,128)(2,1)S(1)}, u32[]{:S(2)}, u32[]{:S(2)}) async-start(bf16[16,64,512]{2,1,0:T(8,128)(2,1)} %bitcast.5), calls=%async_computation | async-start | bytes 2097152 | tf_op jit(solution)/shard_map/gather/all_to_all | solution.py:372
  51.0 16.3 %collective-permute-start.10 = (bf16[256,2048]{1,0:T(8,128)(2,1)}, bf16[256,2048]{1,0:T(8,128)(2,1)}, u32[]{:S(2)}, u32[]{:S(2)}) collective-permute-start(bf16[256,2048]{1,0:T(8,128)(2,1)} %collective-permute-done.8.refs_2_), channel_id=1, source_target_pairs={{0,1},{1,0},{2,3},{3,2},{4,5},{5,4},{6,7},{7,6},{8,9},{9,8},{10,11... | collective-permute-start | bytes 3145736 | tf_op jit(solution)/shard_map/weights/ppermute | solution.py:20
  51.1 16.2 %collective-permute-start.9 = (bf16[512,2048]{1,0:T(8,128)(2,1)}, bf16[512,2048]{1,0:T(8,128)(2,1)S(1)}, u32[]{:S(2)}, u32[]{:S(2)}) collective-permute-start(bf16[512,2048]{1,0:T(8,128)(2,1)} %collective-permute-done.7.refs_0_), channel_id=1, source_target_pairs={{0,1},{1,0},{2,3},{3,2},{4,5},{5,4},{6,7},{7,6},{8,9},{9,8},{10,11... | collective-permute-start | bytes 6291464 | tf_op jit(solution)/shard_map/weights/ppermute | solution.py:20
  65.7 1.0 copy-start
  66.7 0.6 copy-start.2
  67.3 1.3 %copy-start.3 = (bf16[512,2048]{1,0:T(8,128)(2,1)}, bf16[512,2048]{1,0:T(8,128)(2,1)S(1)}, u32[]{:S(2)}) copy-start(bf16[512,2048]{1,0:T(8,128)(2,1)S(1)} %collective-permute-done.9.refs_1_) | copy-start | bytes 6291460
